TPU v7x, 256 devices: a whole 4x4x8 slice. The times are simulated.
256 devices in a mesh: replica: 32 (over y, x, core), tensor: 8 (over z).
Axes of the slice: x: 4, y: 4, z: 8, core: 2. Of those that a mesh axis runs over, the one named last changes fastest.
Arguments:
- x_rows: bfloat16 [4096, 8192], P('replica', 'tensor'), may hold values from -6 to 6
- v_weight: bfloat16 [8192, 1024], P(None, 'tensor'), may hold values from -0.0625 to 0.0625
- home_a: bfloat16 [512, 64, 8192], P('replica', None, 'tensor'), may hold values from -0.0625 to 0.0625
- home_b: bfloat16 [512, 64, 1024], P('replica', None, 'tensor'), may hold values from -0.75 to 0.75
- cache_a: bfloat16 [1536, 64, 8192], P('replica', None, 'tensor'), may hold values from -0.0625 to 0.0625
- cache_b: bfloat16 [1536, 64, 1024], P('replica', None, 'tensor'), may hold values from -0.75 to 0.75
- miss_ids: int32 [32, 32], P('replica'), may hold values from 0 to 511, as said below
- evict_slots: int32 [32, 32], P('replica'), may hold values from 0 to 47, as said below
- slot_ids: int32 [32, 48], P('replica'), may hold values from 0 to 511, as said below
- row_ids: int32 [4096], P('replica'), may hold values from 0 to 511, as said below
Outputs:
- value_out: bfloat16 [4096, 1024], P('replica', 'tensor')
Inputs may be any that keep to these rules, and one draw needn't show every extreme that they name: `miss_ids`: each replica's 32 ids are distinct and none is homed on the replica itself; at most 2 are homed on any one replica, and exactly 2 on some replica in every list. `evict_slots`: each replica's entries are distinct slots. `slot_ids`: the slots that are not evicted hold the 16 adapters homed on the replica itself, each once; evicted slots hold arbitrary ids. `row_ids`: every row names an adapter that its replica holds after the evicted slots are refilled.
All inputs are finite; a program needn't handle non-finite values.
Results may differ from a plain program's by a relative error of at most 0.0046.
Values may be sent and summed in bfloat16 or wider, within the bound.
No kernel may reach another device: no remote copies, remote signals or barrier semaphores. Data moves between devices by JAX's collectives and lax.ppermute only.
A program may use at most 128 MiB of HBM per device.

v0:
```python
import functools

import jax
import jax.numpy as jnp
from jax import lax
from jax.experimental import pallas as pl
from jax.experimental.pallas import tpu as pltpu
from jax.sharding import PartitionSpec as P

adapter_scale = 2.0
room = 16
lanes = 128
bf16, f32, i32 = jnp.bfloat16, jnp.float32, jnp.int32


def call(kernel, out_shape, *args, smem=0, flops=0, limit=32 << 20):
    nbytes = sum(a.size * a.dtype.itemsize for a in args)
    nbytes += sum(o.size * o.dtype.itemsize for o in jax.tree.leaves(out_shape))
    specs = [pl.BlockSpec(memory_space=pltpu.SMEM)] * smem
    specs += [pl.BlockSpec(memory_space=pltpu.VMEM)] * (len(args) - smem)
    return pl.pallas_call(
        kernel,
        out_shape=out_shape,
        in_specs=specs,
        out_specs=jax.tree.map(lambda _: pl.BlockSpec(memory_space=pltpu.VMEM), out_shape),
        compiler_params=pltpu.CompilerParams(vmem_limit_bytes=limit),
        cost_estimate=pl.CostEstimate(flops=flops, bytes_accessed=nbytes, transcendentals=0),
    )(*args)


def column(row):
    n = row.shape[1]
    down = lax.broadcasted_iota(i32, (n, n), 0)
    across = lax.broadcasted_iota(i32, (n, n), 1)
    return jnp.sum(jnp.where(down == across, row, 0), axis=1, keepdims=True)


def targets(ids, me, turn, per_home):
    n = ids.shape[1]
    home = ids // per_home
    down = lax.broadcasted_iota(i32, (n, n), 0)
    across = lax.broadcasted_iota(i32, (n, n), 1)
    before = (column(home) == home) & (down < across)
    rank = jnp.sum(before.astype(i32), axis=0, keepdims=True)
    away = home != me
    most = jnp.max(jnp.where(away, rank + 1, 0))
    place = rank - turn * room
    sent = away & (place >= 0) & (place < room)
    return jnp.where(sent, home * room + place, -1), most


def spread(count, width, inner):
    at = lax.broadcasted_iota(i32, (width, count * inner), 0)
    col = lax.broadcasted_iota(i32, (width, count * inner), 1)
    return (col // inner == at).astype(bf16)


def dot(a, b):
    return jnp.dot(a, b, preferred_element_type=f32)


def dot_t(a, b):
    return lax.dot_general(a, b, (((1,), (1,)), ((), ())), preferred_element_type=f32)


def pack_kernel(per_home, where_ref, ids_ref, x_ref, out_ref):
    slots = out_ref.shape[0]
    width = x_ref.shape[1]
    ids = ids_ref[...]
    n = ids.shape[1]
    to, most = targets(ids, where_ref[0], where_ref[1], per_home)
    place = (lax.broadcasted_iota(i32, (slots, n), 0) == to).astype(bf16)
    out_ref[:, :width] = dot(place, x_ref[...]).astype(bf16)
    lane = lax.broadcasted_iota(i32, (n, lanes), 1)
    which = (lane == column(ids % per_home)).astype(bf16)
    tag = dot(place, which)
    lane = lax.broadcasted_iota(i32, (slots, lanes), 1)
    out_ref[:, width:] = jnp.where(lane == per_home, most.astype(f32), tag).astype(bf16)


def masked_down(x, pick, factors_ref, inner):
    step = 4 * inner
    total = None
    for at in range(0, factors_ref.shape[0], step):
        part = dot_t(x, factors_ref[at : at + step, :]) * pick(at, step)
        part = part[:, : 2 * inner] + part[:, 2 * inner :]
        total = part if total is None else total + part
    return total + pltpu.roll(total, inner, 1)


def fold(both, inner):
    half = both.shape[0] // 2
    lane = lax.broadcasted_iota(i32, (half, 2 * inner), 1)
    return jnp.where(lane < inner, both[:half], both[half:])


def unfold(folded, inner):
    half = folded.shape[0]
    lane = lax.broadcasted_iota(i32, (half, 2 * inner), 1)
    other = pltpu.roll(folded, inner, 1)
    return jnp.concatenate(
        [jnp.where(lane < inner, folded, other), jnp.where(lane < inner, other, folded)], axis=0
    )


def masked_up(both, pick, factors_ref, inner):
    step = 4 * inner
    wide = jnp.concatenate([both, both], axis=1)
    total = None
    for at in range(0, factors_ref.shape[0], step):
        part = dot((wide * pick(at, step)).astype(bf16), factors_ref[at : at + step, :])
        total = part if total is None else total + part
    return total


def picker(onehot, inner):
    width = onehot.shape[1]

    def pick(at, step):
        row = lax.broadcasted_iota(i32, (width, step), 0)
        col = lax.broadcasted_iota(i32, (width, step), 1)
        return dot(onehot, ((col + at) // inner == row).astype(bf16))

    return pick


def own_pick(ids_ref, slot_ref, evict_ref):
    ids = column(ids_ref[...])
    slot = slot_ref[...]
    count = slot.shape[1]
    at = lax.broadcasted_iota(i32, (lanes, lanes), 1)
    listed = column(evict_ref[...])
    gone = jnp.max((listed == lax.broadcasted_iota(i32, (listed.shape[0], count), 1)).astype(i32), axis=0, keepdims=True)
    hit = (ids == slot) & (gone == 0)
    hit = jnp.where(hit, 1.0, 0.0)
    del at
    return jnp.pad(hit, ((0, 0), (0, lanes - count))).astype(bf16)


def own_down_kernel(inner, ids_ref, slot_ref, evict_ref, x_ref, a_ref, out_ref):
    pick = picker(own_pick(ids_ref, slot_ref, evict_ref), inner)
    out_ref[...] = fold(masked_down(x_ref[...], pick, a_ref, inner), inner).astype(bf16)


def down_kernel(inner, got_ref, a_ref, out_ref):
    width = a_ref.shape[1]
    pick = picker(got_ref[:, width:], inner)
    out_ref[...] = fold(masked_down(got_ref[:, :width], pick, a_ref, inner), inner).astype(bf16)


def low_of(parts_ref, lo, hi, inner):
    total = parts_ref[0, lo:hi, :].astype(f32)
    for k in range(1, parts_ref.shape[0]):
        total = total + parts_ref[k, lo:hi, :].astype(f32)
    return unfold(total.astype(bf16).astype(f32), inner)


def up_kernel(inner, parts_ref, tag_ref, b_ref, out_ref):
    half = tag_ref.shape[0] // 2
    both = low_of(parts_ref, 0, half, inner)
    out_ref[...] = masked_up(both, picker(tag_ref[...], inner), b_ref, inner).astype(bf16)


def own_up_kernel(inner, at, ids_ref, slot_ref, evict_ref, parts_ref, b_ref, out_ref):
    pick = picker(own_pick(ids_ref, slot_ref, evict_ref), inner)
    both = low_of(parts_ref, at, parts_ref.shape[1], inner)
    out_ref[...] = masked_up(both, pick, b_ref, inner)


def add_kernel(per_home, where_ref, ids_ref, back_ref, total_ref, out_ref):
    slots = back_ref.shape[0]
    ids = ids_ref[...]
    n = ids.shape[1]
    to, _ = targets(ids, where_ref[0], where_ref[1], per_home)
    place = (lax.broadcasted_iota(i32, (slots, n), 0) == to).astype(bf16)
    came = lax.dot_general(place, back_ref[...], (((0,), (0,)), ((), ())), preferred_element_type=f32)
    out_ref[...] = total_ref[...] + adapter_scale * came


def swap(blocks, axis):
    return lax.all_to_all(blocks, axis, split_axis=0, concat_axis=0, tiled=True)


def shards(
    x_rows, v_weight, home_a, home_b, cache_a, cache_b, miss_ids, evict_slots, slot_ids, row_ids
):
    n, width = x_rows.shape
    per_home, inner, _ = home_a.shape
    cols = home_b.shape[2]
    replicas = lax.axis_size("replica")
    sides = lax.axis_size("tensor")
    slots = replicas * room
    me = lax.axis_index("replica").astype(i32)
    ids = row_ids.reshape(1, n)
    a_all = home_a.reshape(per_home * inner, width)
    b_all = home_b.reshape(per_home * inner, cols)
    kept_a = cache_a.reshape(-1, width)
    kept_b = cache_b.reshape(-1, cols)

    def send(turn):
        where = jnp.stack([me, turn.astype(i32)])
        packed = call(
            functools.partial(pack_kernel, per_home),
            jax.ShapeDtypeStruct((slots, width + lanes), bf16),
            where, ids, x_rows, smem=1, flops=2 * slots * n * width,
        )
        got = swap(packed.reshape(replicas, room, width + lanes), "replica")
        return where, got.reshape(slots, width + lanes)

    def down(got):
        return call(
            functools.partial(down_kernel, inner),
            jax.ShapeDtypeStruct((slots // 2, lanes), bf16),
            got, a_all, flops=2 * slots * width * per_home * inner,
        )

    def share(part):
        return swap(jnp.broadcast_to(part[None], (sides, *part.shape)), "tensor")

    def up(parts, got):
        back = call(
            functools.partial(up_kernel, inner),
            jax.ShapeDtypeStruct((slots, cols), bf16),
            parts, got[:, width:], b_all, flops=2 * slots * cols * per_home * inner,
        )
        return swap(back.reshape(replicas, room, cols), "replica").reshape(slots, cols)

    def add(where, back, total):
        return call(
            functools.partial(add_kernel, per_home),
            jax.ShapeDtypeStruct((n, cols), f32),
            where, ids, back, total, smem=1, flops=2 * slots * n * cols,
        )

    where, got = send(jnp.int32(0))
    whole = lax.all_gather(x_rows, "tensor", axis=1, tiled=True)
    own = call(
        functools.partial(own_down_kernel, inner),
        jax.ShapeDtypeStruct((n // 2, lanes), bf16),
        ids, slot_ids, evict_slots, x_rows, kept_a, flops=2 * n * width * kept_a.shape[0],
    )
    most = jnp.max(got[:, width + per_home].astype(f32)).astype(i32)
    turns = (most + room - 1) // room
    parts = share(jnp.concatenate([down(got), own], axis=0))
    base = jnp.dot(whole, v_weight, preferred_element_type=f32)
    own_lora = call(
        functools.partial(own_up_kernel, inner, slots // 2),
        jax.ShapeDtypeStruct((n, cols), f32),
        ids, slot_ids, evict_slots, parts, kept_b, flops=2 * n * cols * kept_b.shape[0],
    )
    total = add(where, up(parts, got), base + adapter_scale * own_lora)

    def again(state):
        turn, total = state
        where, got = send(turn)
        return turn + 1, add(where, up(share(down(got)), got), total)

    _, total = lax.while_loop(lambda s: s[0] < turns, again, (jnp.int32(1), total))
    return total.astype(bf16)


def solution(mesh):
    return jax.shard_map(
        shards,
        mesh=mesh,
        in_specs=(
            P("replica", "tensor"),
            P(None, "tensor"),
            P("replica", None, "tensor"),
            P("replica", None, "tensor"),
            P("replica", None, "tensor"),
            P("replica", None, "tensor"),
            P("replica", None),
            P("replica", None),
            P("replica", None),
            P("replica"),
        ),
        out_specs=P("replica", "tensor"),
        check_vma=False,
    )
```

profile of v0, /device:TPU:1, one launch (start us, length us, event | category | flops | bytes accessed | tf_op | source)
XLA Modules:
  0.0 94.6 jit_solution(7996341942183656676)
XLA Ops:
  6.5 0.0 all-gather.2.cloned.1.call-start
  6.6 0.7 all-gather.2.cloned.1.call-update
  7.3 0.1 pad_add_fusion.1.where_ref
  7.4 2.6 %shard_map.91 = bf16[512,1152]{1,0:T(8,128)(2,1)} custom-call(s32[2]{0:T(128)S(1)} %pad_add_fusion.1.where_ref, s32[1,128]{1,0:T(1,128)} %bitcast.42, bf16[128,1024]{1,0:T(8,128)(2,1)} %x_ref.3), custom_call_target="tpu_custom_call" | custom-call | flops 134217728 | bytes 1442312 | tf_op jit(solution)/shard_map/pallas_call | solution.py:21
  9.9 8.6 %all-to-all-start.3 = ((bf16[32,16,1152]{2,1,0:T(8,128)(2,1)}), bf16[32,16,1152]{2,1,0:T(8,128)(2,1)S(1)}, u32[]{:S(2)}, u32[]{:S(2)}) async-start(bf16[32,16,1152]{2,1,0:T(8,128)(2,1)} %bitcast.8), calls=%async_computation.3 | async-start | bytes 2359296 | tf_op jit(solution)/shard_map/all_to_all | solution.py:181
  18.6 2.8 %copy-done.2 = bf16[48,64,1024]{2,1,0:T(8,128)(2,1)S(1)} copy-done((bf16[48,64,1024]{2,1,0:T(8,128)(2,1)S(1)}, bf16[48,64,1024]{2,1,0:T(8,128)(2,1)}, u32[]{:S(2)}) %copy-start.2) | copy-done | bytes 6291480
  21.3 3.1 %shard_map.93 = bf16[64,128]{1,0:T(8,128)(2,1)S(1)} custom-call(s32[1,128]{1,0:T(1,128)S(1)} %bitcast.43, s32[1,48]{1,0:T(1,128)S(1)} %copy-done.5, s32[1,32]{1,0:T(1,128)S(1)} %copy-done.6, bf16[128,1024]{1,0:T(8,128)(2,1)} %x_ref.3, bf16[3072,1024]{1,0:T(8,128)(2,1)S(1)} %bitcast.34), custom_call_target="tpu_custom_call" | custom-call | flops 805306368 | bytes 6570816 | tf_op jit(solution)/shard_map/pallas_call | solution.py:21
  24.4 11.8 %all-to-all-done.3 = bf16[32,16,1152]{2,1,0:T(8,128)(2,1)S(1)} async-done(((bf16[32,16,1152]{2,1,0:T(8,128)(2,1)}), bf16[32,16,1152]{2,1,0:T(8,128)(2,1)S(1)}, u32[]{:S(2)}, u32[]{:S(2)}) %all-to-all-start.3) | async-done | bytes 1179680 | tf_op jit(solution)/shard_map/all_to_all | solution.py:181
  36.2 3.6 %shard_map.92 = bf16[256,128]{1,0:T(8,128)(2,1)S(1)} custom-call(bf16[512,1152]{1,0:T(8,128)(2,1)S(1)} %bitcast.35, bf16[1024,1024]{1,0:T(8,128)(2,1)} %bitcast.47), custom_call_target="tpu_custom_call" | custom-call | flops 1073741824 | bytes 3342336 | tf_op jit(solution)/shard_map/pallas_call | solution.py:21
  39.9 0.0 copy-start.8
  39.9 0.9 broadcast_in_dim.4
  40.8 8.2 %all-to-all-start.4 = ((bf16[8,320,128]{2,1,0:T(8,128)(2,1)}), bf16[8,320,128]{2,1,0:T(8,128)(2,1)S(1)}, u32[]{:S(2)}, u32[]{:S(2)}) async-start(bf16[8,320,128]{2,1,0:T(8,128)(2,1)} %broadcast_in_dim.4), calls=%async_computation.4 | async-start | bytes 1310720 | tf_op jit(solution)/shard_map/all_to_all | solution.py:181
  49.0 1.7 %slice_reduce_fusion = bf16[]{:T(256)} fusion(bf16[512,1152]{1,0:T(8,128)(2,1)} %bitcast.36), kind=kLoop, calls=%fused_computation.2 | loop fusion | flops 511 | bytes 1026 | tf_op jit(solution)/shard_map/reduce_max | solution.py:242
  51.3 0.9 slice.12.tag_ref
  52.3 15.5 %all-to-all-done.4.parts_ref = bf16[8,320,128]{2,1,0:T(8,128)(2,1)S(1)} async-done(((bf16[8,320,128]{2,1,0:T(8,128)(2,1)}), bf16[8,320,128]{2,1,0:T(8,128)(2,1)S(1)}, u32[]{:S(2)}, u32[]{:S(2)}) %all-to-all-start.4) | async-done | bytes 655392 | tf_op jit(solution)/shard_map/all_to_all | solution.py:181
  67.8 1.1 %copy-done.4 = bf16[48,64,128]{2,1,0:T(8,128)(2,1)S(1)} copy-done((bf16[48,64,128]{2,1,0:T(8,128)(2,1)S(1)}, bf16[48,64,128]{2,1,0:T(8,128)(2,1)}, u32[]{:S(2)}) %copy-start.4) | copy-done | bytes 786456
  68.9 0.9 shard_map.95
  69.8 1.4 %shard_map.94 = bf16[512,128]{1,0:T(8,128)(2,1)} custom-call(bf16[8,320,128]{2,1,0:T(8,128)(2,1)S(1)} %all-to-all-done.4.parts_ref, bf16[512,128]{1,0:T(8,128)(2,1)S(1)} %slice.12.tag_ref, bf16[1024,128]{1,0:T(8,128)(2,1)S(1)} %bitcast.40), custom_call_target="tpu_custom_call" | custom-call | flops 134217728 | bytes 1179648 | tf_op jit(solution)/shard_map/pallas_call | solution.py:21
  71.1 7.5 %all-to-all-start.5 = ((bf16[32,16,128]{2,1,0:T(8,128)(2,1)}), bf16[32,16,128]{2,1,0:T(8,128)(2,1)S(1)}, u32[]{:S(2)}, u32[]{:S(2)}) async-start(bf16[32,16,128]{2,1,0:T(8,128)(2,1)} %bitcast.13), calls=%async_computation.5 | async-start | bytes 262144 | tf_op jit(solution)/shard_map/all_to_all | solution.py:181
  78.6 0.0 all-gather.2.cloned.1.call-done
  78.6 2.3 %convolution_add_fusion.total_ref = f32[128,128]{1,0:T(8,128)S(1)} fusion(bf16[128,8192]{1,0:T(8,128)(2,1)} %all-gather.2.cloned.1.call-done, bf16[8192,128]{1,0:T(8,128)(2,1)S(1)} %copy-done, f32[128,128]{1,0:T(8,128)S(1)} %shard_map.95), kind=kOutput, calls=%fused_computation.1 | convolution fusion | flops 268468224 | bytes 4325376 | tf_op jit(solution)/shard_map/dot_general | solution.py:245
  81.0 5.2 %all-to-all-done.5 = bf16[32,16,128]{2,1,0:T(8,128)(2,1)S(1)} async-done(((bf16[32,16,128]{2,1,0:T(8,128)(2,1)}), bf16[32,16,128]{2,1,0:T(8,128)(2,1)S(1)}, u32[]{:S(2)}, u32[]{:S(2)}) %all-to-all-start.5) | async-done | bytes 131104 | tf_op jit(solution)/shard_map/all_to_all | solution.py:181
  86.2 0.9 shard_map.96
  87.2 0.6 convert_element_type.8
  (17 shorter events, 0.1 us)
Async XLA Ops:
  6.5 72.1 %copy-start = (bf16[8192,128]{1,0:T(8,128)(2,1)S(1)}, bf16[8192,128]{1,0:T(8,128)(2,1)}, u32[]{:S(2)}) copy-start(bf16[8192,128]{1,0:T(8,128)(2,1)} %param.13) | copy-start | bytes 6291460
  6.5 12.0 %copy-start.9 = (s32[128]{0:T(128)S(1)}, s32[128]{0:T(128)}, u32[]{:S(2)}) copy-start(s32[128]{0:T(128)} %param.20) | copy-start | bytes 1540
  6.5 12.0 %copy-start.6 = (s32[1,32]{1,0:T(1,128)S(1)}, s32[1,32]{1,0:T(1,128)}, u32[]{:S(2)}) copy-start(s32[1,32]{1,0:T(1,128)} %evict_ref.3) | copy-start | bytes 388
  6.5 12.0 %copy-start.5 = (s32[1,48]{1,0:T(1,128)S(1)}, s32[1,48]{1,0:T(1,128)}, u32[]{:S(2)}) copy-start(s32[1,48]{1,0:T(1,128)} %slot_ref.3) | copy-start | bytes 580
  6.5 72.1 %all-gather.2.cloned.1.call-start = ((), (), s32[]{:S(2)}) async-start(), calls=%async_computation.6 | async-start | bytes 2359296 | tf_op jit(solution)/shard_map/all_gather | solution.py:236
  9.9 26.3 %all-to-all-start.3 = ((bf16[32,16,1152]{2,1,0:T(8,128)(2,1)}), bf16[32,16,1152]{2,1,0:T(8,128)(2,1)S(1)}, u32[]{:S(2)}, u32[]{:S(2)}) async-start(bf16[32,16,1152]{2,1,0:T(8,128)(2,1)} %bitcast.8), calls=%async_computation.3 | async-start | bytes 2359296 | tf_op jit(solution)/shard_map/all_to_all | solution.py:181
  18.6 2.8 %copy-start.2 = (bf16[48,64,1024]{2,1,0:T(8,128)(2,1)S(1)}, bf16[48,64,1024]{2,1,0:T(8,128)(2,1)}, u32[]{:S(2)}) copy-start(bf16[48,64,1024]{2,1,0:T(8,128)(2,1)} %param.16) | copy-start | bytes 18874372
  36.2 4.6 %copy-start.3 = (bf16[32,16,1152]{2,1,0:T(8,128)(2,1)}, bf16[32,16,1152]{2,1,0:T(8,128)(2,1)S(1)}, u32[]{:S(2)}) copy-start(bf16[32,16,1152]{2,1,0:T(8,128)(2,1)S(1)} %all-to-all-done.3) | copy-start | bytes 3538948
  39.9 29.9 %copy-start.8 = (bf16[16,64,128]{2,1,0:T(8,128)(2,1)S(1)}, bf16[16,64,128]{2,1,0:T(8,128)(2,1)}, u32[]{:S(2)}) copy-start(bf16[16,64,128]{2,1,0:T(8,128)(2,1)} %param.15) | copy-start | bytes 786436
  40.8 26.9 %all-to-all-start.4 = ((bf16[8,320,128]{2,1,0:T(8,128)(2,1)}), bf16[8,320,128]{2,1,0:T(8,128)(2,1)S(1)}, u32[]{:S(2)}, u32[]{:S(2)}) async-start(bf16[8,320,128]{2,1,0:T(8,128)(2,1)} %broadcast_in_dim.4), calls=%async_computation.4 | async-start | bytes 1310720 | tf_op jit(solution)/shard_map/all_to_all | solution.py:181
  67.8 1.1 %copy-start.4 = (bf16[48,64,128]{2,1,0:T(8,128)(2,1)S(1)}, bf16[48,64,128]{2,1,0:T(8,128)(2,1)}, u32[]{:S(2)}) copy-start(bf16[48,64,128]{2,1,0:T(8,128)(2,1)} %param.17) | copy-start | bytes 2359300
  71.1 15.1 %all-to-all-start.5 = ((bf16[32,16,128]{2,1,0:T(8,128)(2,1)}), bf16[32,16,128]{2,1,0:T(8,128)(2,1)S(1)}, u32[]{:S(2)}, u32[]{:S(2)}) async-start(bf16[32,16,128]{2,1,0:T(8,128)(2,1)} %bitcast.13), calls=%async_computation.5 | async-start | bytes 262144 | tf_op jit(solution)/shard_map/all_to_all | solution.py:181
  78.6 8.5 %copy-start.7 = (bf16[128,1024]{1,0:T(8,128)(2,1)S(1)}, bf16[128,1024]{1,0:T(8,128)(2,1)}, u32[]{:S(2)}) copy-start(bf16[128,1024]{1,0:T(8,128)(2,1)} %x_ref.3) | copy-start | bytes 786436
Sparse Core Ops, SparseCore 0:
  9.2 41.2 all-gather.1
where the time goes:
time: 95.2 us; the launch traced here: 94.6 us
  waiting for transfers between devices  33.3 us (35%)
  starting transfers between devices  24.3 us (26%)
  between operations  14.2 us (15%)
  Pallas kernels  12.4 us (13%)
  local copies, waits for them, and re-layouts  5.79 us (6%)
  other arithmetic  2.38 us (2%)
  matrix products  2.32 us (2%)
    all_to_all x3, waiting for transfers between devices, swap(): return lax.all_to_all(blocks, axis, split_axis=0, concat_axis=0, tiled=True)  32.5 us
    all_to_all x3, starting transfers between devices, swap(): return lax.all_to_all(blocks, axis, split_axis=0, concat_axis=0, tiled=True)  24.2 us
    pallas_call x6, Pallas kernels, call(): pl.pallas_call(kernel, out_shape=out_shape, in_specs=specs, out_specs=jax...  12.4 us
    unnamed x18, local copies, waits for them, and re-layouts  3.94 us
    dot_general x1, matrix products, shards(): base = jnp.dot(whole, v_weight, preferred_element_type=f32)  2.32 us
  transfers between devices with their start and end apart: 4, of which 3 were waited for; matrix products, arithmetic and copies ran while one was open for 6% of the time, Pallas kernels for 12%

commit v1 on v0

v1 whole, which is shorter than its diff:
```python
import functools

import jax
import jax.numpy as jnp
from jax import lax
from jax.experimental import pallas as pl
from jax.experimental.pallas import tpu as pltpu
from jax.sharding import PartitionSpec as P

adapter_scale = 2.0
room = 16
fits = 160
first_count = 64
lanes = 128
bf16, f32, i32 = jnp.bfloat16, jnp.float32, jnp.int32


def call(kernel, out_shape, *args, smem=0, smem_out=0, us=1, limit=8 << 20):
    scalar, whole = pl.BlockSpec(memory_space=pltpu.SMEM), pl.BlockSpec(memory_space=pltpu.VMEM)
    several = isinstance(out_shape, tuple)
    results = len(out_shape) if several else 1
    out_specs = (whole,) * (results - smem_out) + (scalar,) * smem_out
    return pl.pallas_call(
        kernel,
        out_shape=out_shape,
        in_specs=[scalar] * smem + [whole] * (len(args) - smem),
        out_specs=out_specs if several else out_specs[0],
        compiler_params=pltpu.CompilerParams(vmem_limit_bytes=limit),
        cost_estimate=pl.CostEstimate(flops=0, bytes_accessed=us * 3_000_000, transcendentals=0),
    )(*args)


def column(row):
    n = row.shape[1]
    down = lax.broadcasted_iota(i32, (n, n), 0)
    across = lax.broadcasted_iota(i32, (n, n), 1)
    return jnp.sum(jnp.where(down == across, row, 0), axis=1, keepdims=True)


def ranks(home, todo):
    n = home.shape[1]
    down = lax.broadcasted_iota(i32, (n, n), 0)
    across = lax.broadcasted_iota(i32, (n, n), 1)
    before = (column(home) == home) & (column(todo) > 0) & (down < across)
    return jnp.sum(before.astype(i32), axis=0, keepdims=True)


def targets(home, todo):
    rank = ranks(home, todo)
    return jnp.where((todo > 0) & (rank < room), home * room + rank, -1)


def dot(a, b):
    return jnp.dot(a, b, preferred_element_type=f32)


def dot_t(a, b):
    return lax.dot_general(a, b, (((1,), (1,)), ((), ())), preferred_element_type=f32)


def pack_kernel(per_home, me_ref, ids_ref, todo_ref, x_ref, out_ref):
    slots = out_ref.shape[0]
    width = x_ref.shape[1]
    ids = ids_ref[...]
    n = ids.shape[1]
    home = ids // per_home
    todo = jnp.where(home != me_ref[0], todo_ref[...], 0)
    to = targets(home, todo)
    place = (lax.broadcasted_iota(i32, (slots, n), 0) == to).astype(bf16)
    out_ref[:, :width] = dot(place, x_ref[...]).astype(bf16)
    lane = lax.broadcasted_iota(i32, (n, lanes), 1)
    which = (lane == column(ids % per_home)).astype(bf16)
    tag = dot(place, which)
    wanted = (lane == column(home) + first_count) & (column(todo) > 0)
    counts = jnp.sum(wanted.astype(f32), axis=0, keepdims=True)
    lane = lax.broadcasted_iota(i32, (slots, lanes), 1)
    out_ref[:, width:] = jnp.where(lane >= first_count, counts, tag).astype(bf16)


def left_kernel(per_home, fits, me_ref, ids_ref, count_ref, todo_ref, turns_ref):
    ids = ids_ref[...]
    home = ids // per_home
    away = home != me_ref[0]
    todo = away.astype(i32)
    counts = count_ref[...]
    replicas = counts.shape[0]
    sent = jnp.minimum(counts, float(room))
    down = lax.broadcasted_iota(i32, (replicas, replicas), 0)
    across = lax.broadcasted_iota(i32, (replicas, replicas), 1)
    ahead = dot((across < down).astype(bf16), sent.astype(bf16))
    left = counts - jnp.clip(float(fits) - ahead, 0.0, sent)
    lane = lax.broadcasted_iota(i32, (replicas, lanes), 1)
    most = jnp.max(jnp.where(lane >= first_count, left, 0.0)).astype(i32)
    turns_ref[0] = (most + room - 1) // room
    mine = lax.broadcasted_iota(i32, (replicas, lanes), 0) == me_ref[0]
    mine = jnp.sum(jnp.where(mine, ahead, 0.0), axis=0, keepdims=True).astype(i32)
    at = lax.broadcasted_iota(i32, (lanes, home.shape[1]), 0)
    mine = jnp.sum(jnp.where(at == home + first_count, column(mine), 0), axis=0, keepdims=True)
    rank = ranks(home, todo)
    served = (rank < room) & (mine + rank < fits)
    todo_ref[...] = jnp.where(away & ~served, 1, 0)


def masked_down(x, pick, factors_ref, inner):
    step = 4 * inner
    total = None
    for at in range(0, factors_ref.shape[0], step):
        part = dot_t(x, factors_ref[at : at + step, :]) * pick(at, step)
        part = part[:, : 2 * inner] + part[:, 2 * inner :]
        total = part if total is None else total + part
    return total + pltpu.roll(total, inner, 1)


def fold(both, inner):
    half = both.shape[0] // 2
    lane = lax.broadcasted_iota(i32, (half, 2 * inner), 1)
    return jnp.where(lane < inner, both[:half], both[half:])


def unfold(folded, inner):
    half = folded.shape[0]
    lane = lax.broadcasted_iota(i32, (half, 2 * inner), 1)
    other = pltpu.roll(folded, inner, 1)
    return jnp.concatenate(
        [jnp.where(lane < inner, folded, other), jnp.where(lane < inner, other, folded)], axis=0
    )


def masked_up(both, pick, factors_ref, inner):
    step = 4 * inner
    wide = jnp.concatenate([both, both], axis=1)
    total = None
    for at in range(0, factors_ref.shape[0], step):
        part = dot((wide * pick(at, step)).astype(bf16), factors_ref[at : at + step, :])
        total = part if total is None else total + part
    return total


def picker(onehot, inner):
    width = onehot.shape[1]

    def pick(at, step):
        row = lax.broadcasted_iota(i32, (width, step), 0)
        col = lax.broadcasted_iota(i32, (width, step), 1)
        return dot(onehot, ((col + at) // inner == row).astype(bf16))

    return pick


def own_pick(ids_ref, slot_ref, evict_ref):
    ids = column(ids_ref[...])
    slot = slot_ref[...]
    count = slot.shape[1]
    listed = column(evict_ref[...])
    gone = jnp.max((listed == lax.broadcasted_iota(i32, (listed.shape[0], count), 1)).astype(i32), axis=0, keepdims=True)
    hit = (ids == slot) & (gone == 0)
    hit = jnp.where(hit, 1.0, 0.0)
    return jnp.pad(hit, ((0, 0), (0, lanes - count))).astype(bf16)


def own_down_kernel(inner, ids_ref, slot_ref, evict_ref, x_ref, a_ref, out_ref):
    pick = picker(own_pick(ids_ref, slot_ref, evict_ref), inner)
    out_ref[...] = fold(masked_down(x_ref[...], pick, a_ref, inner), inner).astype(bf16)


def kept_slots(at_ref, held):
    at = at_ref[...]
    return (lax.broadcasted_iota(i32, (held, at.shape[1]), 0) == at).astype(bf16)


def down_kernel(inner, per_home, got_ref, a_ref, *refs):
    own_ref = refs[0] if len(refs) == 5 else None
    out_ref, name_ref, at_ref, count_ref = refs[-4:]
    slots = got_ref.shape[0]
    width = a_ref.shape[1]
    held = name_ref.shape[0]
    tag = got_ref[:, width:]
    lane = lax.broadcasted_iota(i32, (16, lanes), 1)
    full = dot_t((lane < per_home).astype(bf16), tag)
    down = lax.broadcasted_iota(i32, (slots, slots), 0)
    across = lax.broadcasted_iota(i32, (slots, slots), 1)
    at = dot(full.astype(bf16), (down < across).astype(bf16))
    at_ref[...] = jnp.where(full > 0.5, at, -1.0)[:1].astype(i32)
    keep = kept_slots(at_ref, held)
    x = dot(keep, got_ref[:, :width]).astype(bf16)
    name = dot(keep, tag)
    lane = lax.broadcasted_iota(i32, (held, lanes), 1)
    name = jnp.where(lane < per_home, name, 0.0).astype(bf16)
    name_ref[...] = name
    part = fold(masked_down(x, picker(name, inner), a_ref, inner), inner).astype(bf16)
    for side in range(out_ref.shape[0]):
        out_ref[side, : held // 2, :] = part
        if own_ref is not None:
            out_ref[side, held // 2 :, :] = own_ref[...]
    for r in range(count_ref.shape[0]):
        count_ref[r : r + 1, :] = got_ref[r * room : r * room + 1, width:].astype(f32)


def low_of(parts_ref, lo, hi, inner):
    total = parts_ref[0, lo:hi, :].astype(f32)
    for k in range(1, parts_ref.shape[0]):
        total = total + parts_ref[k, lo:hi, :].astype(f32)
    return unfold(total.astype(bf16).astype(f32), inner)


def up_kernel(inner, parts_ref, name_ref, at_ref, b_ref, out_ref):
    keep = kept_slots(at_ref, name_ref.shape[0])
    half = name_ref.shape[0] // 2
    both = low_of(parts_ref, 0, half, inner)
    lora = masked_up(both, picker(name_ref[...], inner), b_ref, inner).astype(bf16)
    back = lax.dot_general(keep, lora, (((0,), (0,)), ((), ())), preferred_element_type=f32)
    out_ref[...] = back.astype(bf16)


def own_up_kernel(inner, at, ids_ref, slot_ref, evict_ref, parts_ref, b_ref, out_ref):
    pick = picker(own_pick(ids_ref, slot_ref, evict_ref), inner)
    both = low_of(parts_ref, at, parts_ref.shape[1], inner)
    out_ref[...] = masked_up(both, pick, b_ref, inner)


def base_kernel(steps, side_ref, w_ref, *refs):
    *total, out_ref = refs
    blocks = total[-len(steps) :]
    sum_ = total[0][...] if len(total) > len(steps) else None
    width = blocks[0].shape[1]
    sides = w_ref.shape[0] // width
    for block, step in zip(blocks, steps, strict=True):
        side = lax.rem(side_ref[0] + step, sides)
        weight = w_ref[pl.ds(pl.multiple_of(side * width, width), width), :]
        part = dot(block[...], weight)
        sum_ = part if sum_ is None else sum_ + part
    out_ref[...] = sum_


def came_back(per_home, me_ref, ids_ref, todo_ref, back_ref):
    slots = back_ref.shape[0]
    home = ids_ref[...] // per_home
    todo = jnp.where(home != me_ref[0], todo_ref[...], 0)
    place = (lax.broadcasted_iota(i32, (slots, home.shape[1]), 0) == targets(home, todo)).astype(bf16)
    return lax.dot_general(place, back_ref[...], (((0,), (0,)), ((), ())), preferred_element_type=f32)


def last_kernel(per_home, me_ref, ids_ref, todo_ref, back_ref, base_ref, own_ref, more_ref, out_ref):
    came = came_back(per_home, me_ref, ids_ref, todo_ref, back_ref)
    lora = own_ref[...] + more_ref[...] + came
    out_ref[...] = (base_ref[...] + adapter_scale * lora).astype(bf16)


def more_kernel(per_home, me_ref, ids_ref, todo_ref, back_ref, more_ref, out_ref, left_ref):
    out_ref[...] = more_ref[...] + came_back(per_home, me_ref, ids_ref, todo_ref, back_ref)
    home = ids_ref[...] // per_home
    todo = todo_ref[...]
    left_ref[...] = jnp.where(ranks(home, todo) < room, 0, todo)


def swap(blocks, axis):
    return lax.all_to_all(blocks, axis, split_axis=0, concat_axis=0, tiled=True)


def shards(
    x_rows, v_weight, home_a, home_b, cache_a, cache_b, miss_ids, evict_slots, slot_ids, row_ids
):
    n, width = x_rows.shape
    per_home, inner, _ = home_a.shape
    cols = home_b.shape[2]
    replicas = lax.axis_size("replica")
    sides = lax.axis_size("tensor")
    slots = replicas * room
    me = lax.axis_index("replica").astype(i32).reshape(1)
    side = lax.axis_index("tensor").astype(i32).reshape(1)
    ids = row_ids.reshape(1, n)
    a_all = home_a.reshape(per_home * inner, width)
    b_all = home_b.reshape(per_home * inner, cols)

    def send(todo):
        packed = call(
            functools.partial(pack_kernel, per_home),
            jax.ShapeDtypeStruct((slots, width + lanes), bf16),
            me, ids, todo, x_rows, smem=1, us=3,
        )
        got = swap(packed.reshape(replicas, room, width + lanes), "replica")
        return got.reshape(slots, width + lanes)

    def down(got, held, *own):
        rows = held // 2 + sum(o.shape[0] for o in own)
        out = (
            jax.ShapeDtypeStruct((sides, rows, lanes), bf16),
            jax.ShapeDtypeStruct((held, lanes), bf16),
            jax.ShapeDtypeStruct((1, slots), i32),
            jax.ShapeDtypeStruct((replicas, lanes), f32),
        )
        return call(functools.partial(down_kernel, inner, per_home), out, got, a_all, *own, us=3)

    def up(parts, name, at):
        return call(
            functools.partial(up_kernel, inner),
            jax.ShapeDtypeStruct((slots, cols), bf16),
            parts, name, at, b_all, us=2,
        )

    def give(back):
        return swap(back.reshape(replicas, room, cols), "replica").reshape(slots, cols)

    todo = jnp.ones((1, n), i32)
    got = send(todo)
    own = call(
        functools.partial(own_down_kernel, inner),
        jax.ShapeDtypeStruct((n // 2, lanes), bf16),
        ids, slot_ids, evict_slots, x_rows, cache_a.reshape(-1, width), us=3, limit=16 << 20,
    )

    def shift(block, by):
        return lax.ppermute(block, "tensor", [(k, (k + by) % sides) for k in range(sides)])

    def base(total, home_step, blocks):
        steps = tuple(s % sides for s in home_step)
        return call(
            functools.partial(base_kernel, steps), jax.ShapeDtypeStruct((n, cols), f32),
            side, v_weight, *total, *blocks, smem=1,
        )

    near = [shift(x_rows, step) for step in (1, -1, 2, -2)]
    part, name, at, counts = down(got, fits, own)
    part, *near = lax.optimization_barrier((part, *near))
    parts = swap(part, "tensor")
    far = [shift(near[2], 1), shift(near[3], -1), shift(near[2], 2)]
    frozen = base((), (0, -1, 1, -2, 2), (x_rows, *near))
    unserved, turns = call(
        functools.partial(left_kernel, per_home, fits),
        (jax.ShapeDtypeStruct((1, n), i32), jax.ShapeDtypeStruct((1,), i32)),
        me, ids, counts, smem=1, smem_out=1, us=2,
    )
    parts, frozen, unserved, turns = lax.optimization_barrier((parts, frozen, unserved, turns))
    back = give(up(parts, name, at))
    own_lora = call(
        functools.partial(own_up_kernel, inner, fits // 2),
        jax.ShapeDtypeStruct((n, cols), f32),
        ids, slot_ids, evict_slots, parts, cache_b.reshape(-1, cols),
    )
    frozen = base((frozen,), (-3, 3, 4), far)
    unserved, turns, back = lax.optimization_barrier((unserved, turns, back))

    def again(state):
        turn, unserved, more = state
        part, name, at, _ = down(send(unserved), slots)
        back = give(up(swap(part, "tensor"), name, at))
        more, unserved = call(
            functools.partial(more_kernel, per_home),
            (jax.ShapeDtypeStruct((n, cols), f32), jax.ShapeDtypeStruct((1, n), i32)),
            me, ids, unserved, back, more, smem=1,
        )
        return turn + 1, unserved, more

    state = (jnp.int32(0), unserved, jnp.zeros((n, cols), f32))
    _, _, more = lax.while_loop(lambda s: s[0] < turns[0], again, state)
    return call(
        functools.partial(last_kernel, per_home),
        jax.ShapeDtypeStruct((n, cols), bf16),
        me, ids, todo, back, frozen, own_lora, more, smem=1,
    )


def solution(mesh):
    return jax.shard_map(
        shards,
        mesh=mesh,
        in_specs=(
            P("replica", "tensor"),
            P(None, "tensor"),
            P("replica", None, "tensor"),
            P("replica", None, "tensor"),
            P("replica", None, "tensor"),
            P("replica", None, "tensor"),
            P("replica", None),
            P("replica", None),
            P("replica", None),
            P("replica"),
        ),
        out_specs=P("replica", "tensor"),
        check_vma=False,
    )
```

time: 95.2 us -> 73.9 us (0.78)
  waiting for transfers between devices: 33.3 us -> 12.8 us
  starting transfers between devices: 24.3 us -> 38.9 us
  between operations: 14.2 us -> 0.15 us
  Pallas kernels: 12.4 us -> 17.2 us
  other arithmetic: 2.38 us -> 0 us
  matrix products: 2.32 us -> 0 us
  local copies, waits for them, and re-layouts: 5.79 us -> 3.53 us
    all_to_all x3, waiting for transfers between devices: 32.5 us -> 11.7 us  [swap(): return lax.all_to_all(blocks, axis, split_axis=0, concat_axis=0, tiled=True)]
    ppermute x0 -> x7, starting transfers between devices: none -> 13.1 us  [shift(): lax.ppermute(block, 'tensor', [(k, (k + by) % sides) for k in range(sides)])]
    pallas_call x6 -> x9, Pallas kernels: 12.4 us -> 17.2 us  [call(): pl.pallas_call(kernel, out_shape=out_shape, in_specs=[scalar] * smem + [w...]
    dot_general x1 -> x0, matrix products: 2.32 us -> none  [shards(): base = jnp.dot(whole, v_weight, preferred_element_type=f32)]
    reduce_max x1 -> x0, other arithmetic: 1.68 us -> none  [shards(): most = jnp.max(got[:, width + per_home].astype(f32)).astype(i32)]
    all_to_all x3, starting transfers between devices: 24.2 us -> 25.7 us  [swap(): return lax.all_to_all(blocks, axis, split_axis=0, concat_axis=0, tiled=True)]
    ppermute x0 -> x7, waiting for transfers between devices: none -> 1.1 us  [shift(): lax.ppermute(block, 'tensor', [(k, (k + by) % sides) for k in range(sides)])]
    unnamed x18 -> x16, local copies, waits for them, and re-layouts: 3.94 us -> 3.52 us
  transfers between devices with their start and end apart: 4 -> 10, of which waited for: 3 -> 4; matrix products, arithmetic and copies ran while one was open for 6% -> 0% of each run, Pallas kernels for 12% -> 19%
where the time goes in v1:
time: 73.9 us; the launch traced here: 73.3 us
  starting transfers between devices  38.9 us (53%)
  Pallas kernels  17.2 us (23%)
  waiting for transfers between devices  12.8 us (17%)
  local copies, waits for them, and re-layouts  3.53 us (5%)
  loops' own time  0.75 us (1%)
    all_to_all x3, starting transfers between devices, swap(): return lax.all_to_all(blocks, axis, split_axis=0, concat_axis=0, tiled=True)  25.7 us
    pallas_call x9, Pallas kernels, call(): pl.pallas_call(kernel, out_shape=out_shape, in_specs=[scalar] * smem + [w...  17.2 us
    ppermute x7, starting transfers between devices, shift(): lax.ppermute(block, 'tensor', [(k, (k + by) % sides) for k in range(sides)])  13.1 us
    all_to_all x3, waiting for transfers between devices, swap(): return lax.all_to_all(blocks, axis, split_axis=0, concat_axis=0, tiled=True)  11.7 us
    unnamed x16, local copies, waits for them, and re-layouts  3.52 us
  transfers between devices with their start and end apart: 10, of which 4 were waited for; matrix products, arithmetic and copies ran while one was open for 0% of the time, Pallas kernels for 19%

profile of v1, /device:TPU:1, one launch (start us, length us, event | category | flops | bytes accessed | tf_op | source)
XLA Modules:
  0.0 73.3 jit_solution(12235706045221238000)
XLA Ops:
  0.0 2.6 %shard_map.91 = bf16[512,1152]{1,0:T(8,128)(2,1)} custom-call(s32[1]{0:T(128)} %bitcast.5.me_ref, s32[1,128]{1,0:T(1,128)} %bitcast.36, s32[1,128]{1,0:T(1,128)S(1)} %broadcast_in_dim.6.todo_ref, bf16[128,1024]{1,0:T(8,128)(2,1)} %refs_0_.1), custom_call_target="tpu_custom_call" | custom-call | bytes 9000000 | tf_op jit(solution)/shard_map/pallas_call | solution.py:23
  2.6 8.7 %all-to-all-start.3 = ((bf16[32,16,1152]{2,1,0:T(8,128)(2,1)}), bf16[32,16,1152]{2,1,0:T(8,128)(2,1)S(1)}, u32[]{:S(2)}, u32[]{:S(2)}) async-start(bf16[32,16,1152]{2,1,0:T(8,128)(2,1)} %bitcast.7), calls=%async_computation.3 | async-start | bytes 2359296 | tf_op jit(solution)/shard_map/all_to_all | solution.py:257
  11.4 1.7 %collective-permute-start = (bf16[128,1024]{1,0:T(8,128)(2,1)}, bf16[128,1024]{1,0:T(8,128)(2,1)}, u32[]{:S(2)}, u32[]{:S(2)}) collective-permute-start(bf16[128,1024]{1,0:T(8,128)(2,1)} %refs_0_.1), channel_id=1, source_target_pairs={{0,1},{1,2},{2,3},{3,4},{4,5},{5,6},{6,7},{7,0},{8,9},{9,10},{10,1... | collective-permute-start | bytes 786440 | tf_op jit(solution)/shard_map/ppermute | solution.py:313
  13.1 4.0 %collective-permute-start.1 = (bf16[128,1024]{1,0:T(8,128)(2,1)}, bf16[128,1024]{1,0:T(8,128)(2,1)}, u32[]{:S(2)}, u32[]{:S(2)}) collective-permute-start(bf16[128,1024]{1,0:T(8,128)(2,1)} %refs_0_.1), channel_id=1, source_target_pairs={{0,7},{1,0},{2,1},{3,2},{4,3},{5,4},{6,5},{7,6},{8,15},{9,8},{10,9... | collective-permute-start | bytes 786440 | tf_op jit(solution)/shard_map/ppermute | solution.py:313
  17.1 3.6 %collective-permute-start.3 = (bf16[128,1024]{1,0:T(8,128)(2,1)}, bf16[128,1024]{1,0:T(8,128)(2,1)}, u32[]{:S(2)}, u32[]{:S(2)}) collective-permute-start(bf16[128,1024]{1,0:T(8,128)(2,1)} %refs_0_.1), channel_id=1, source_target_pairs={{0,6},{1,7},{2,0},{3,1},{4,2},{5,3},{6,4},{7,5},{8,14},{9,15},{10,... | collective-permute-start | bytes 786440 | tf_op jit(solution)/shard_map/ppermute | solution.py:313
  20.7 2.8 %copy-done.1 = bf16[48,64,1024]{2,1,0:T(8,128)(2,1)S(1)} copy-done((bf16[48,64,1024]{2,1,0:T(8,128)(2,1)S(1)}, bf16[48,64,1024]{2,1,0:T(8,128)(2,1)}, u32[]{:S(2)}) %copy-start.1) | copy-done | bytes 6291480
  23.5 3.1 %shard_map.92.refs_0_ = bf16[64,128]{1,0:T(8,128)(2,1)S(1)} custom-call(s32[1,128]{1,0:T(1,128)S(1)} %bitcast.37, s32[1,48]{1,0:T(1,128)S(1)} %copy-done.4, s32[1,32]{1,0:T(1,128)S(1)} %copy-done.5, bf16[128,1024]{1,0:T(8,128)(2,1)} %refs_0_.1, bf16[3072,1024]{1,0:T(8,128)(2,1)S(1)} %bitcast.28), custom_call_target="tpu_custom_call" | custom-call | bytes 9000000 | tf_op jit(solution)/shard_map/pallas_call | solution.py:23
  26.6 2.5 %all-to-all-done.3 = bf16[32,16,1152]{2,1,0:T(8,128)(2,1)S(1)} async-done(((bf16[32,16,1152]{2,1,0:T(8,128)(2,1)}), bf16[32,16,1152]{2,1,0:T(8,128)(2,1)S(1)}, u32[]{:S(2)}, u32[]{:S(2)}) %all-to-all-start.3) | async-done | bytes 1179680 | tf_op jit(solution)/shard_map/all_to_all | solution.py:257
  29.0 3.3 %shard_map.93 = (bf16[8,144,128]{2,1,0:T(8,128)(2,1)S(1)}, bf16[160,128]{1,0:T(8,128)(2,1)S(1)}, s32[1,512]{1,0:T(1,128)S(1)}, f32[32,128]{1,0:T(8,128)S(1)}) custom-call(bf16[512,1152]{1,0:T(8,128)(2,1)S(1)} %bitcast.29, bf16[1024,1024]{1,0:T(8,128)(2,1)} %bitcast.32, bf16[64,128]{1,0:T(8,128)(2,1)S(1)} %shard_map.92.refs_0_), custom_call_target="tpu_custom_call" | custom-call | bytes 9000000 | tf_op jit(solution)/shard_map/pallas_call | solution.py:23
  33.1 1.1 %collective-permute-done.3.refs_4_ = bf16[128,1024]{1,0:T(8,128)(2,1)} collective-permute-done((bf16[128,1024]{1,0:T(8,128)(2,1)}, bf16[128,1024]{1,0:T(8,128)(2,1)}, u32[]{:S(2)}, u32[]{:S(2)}) %collective-permute-start.3) | collective-permute-done | bytes 262176 | tf_op jit(solution)/shard_map/ppermute | solution.py:313
  34.1 7.1 %all-to-all-start.4 = ((bf16[8,144,128]{2,1,0:T(8,128)(2,1)}), bf16[8,144,128]{2,1,0:T(8,128)(2,1)S(1)}, u32[]{:S(2)}, u32[]{:S(2)}) async-start(bf16[8,144,128]{2,1,0:T(8,128)(2,1)} %copy-done.3), calls=%async_computation.4 | async-start | bytes 589824 | tf_op jit(solution)/shard_map/all_to_all | solution.py:257
  41.3 1.5 %collective-permute-start.4 = (bf16[128,1024]{1,0:T(8,128)(2,1)}, bf16[128,1024]{1,0:T(8,128)(2,1)}, u32[]{:S(2)}, u32[]{:S(2)}) collective-permute-start(bf16[128,1024]{1,0:T(8,128)(2,1)} %collective-permute-done.2.refs_3_), channel_id=1, source_target_pairs={{0,1},{1,2},{2,3},{3,4},{4,5},{5,6},{6,7},{7,0},{8,9},{9,10},{10,1... | collective-permute-start | bytes 786440 | tf_op jit(solution)/shard_map/ppermute | solution.py:313
  42.7 1.2 %collective-permute-start.5 = (bf16[128,1024]{1,0:T(8,128)(2,1)}, bf16[128,1024]{1,0:T(8,128)(2,1)}, u32[]{:S(2)}, u32[]{:S(2)}) collective-permute-start(bf16[128,1024]{1,0:T(8,128)(2,1)} %collective-permute-done.3.refs_4_), channel_id=1, source_target_pairs={{0,7},{1,0},{2,1},{3,2},{4,3},{5,4},{6,5},{7,6},{8,15},{9,8},{10,9... | collective-permute-start | bytes 786440 | tf_op jit(solution)/shard_map/ppermute | solution.py:313
  44.0 1.1 %collective-permute-start.6 = (bf16[128,1024]{1,0:T(8,128)(2,1)}, bf16[128,1024]{1,0:T(8,128)(2,1)}, u32[]{:S(2)}, u32[]{:S(2)}) collective-permute-start(bf16[128,1024]{1,0:T(8,128)(2,1)} %collective-permute-done.2.refs_3_), channel_id=1, source_target_pairs={{0,2},{1,3},{2,4},{3,5},{4,6},{5,7},{6,0},{7,1},{8,10},{9,11},{10,... | collective-permute-start | bytes 786440 | tf_op jit(solution)/shard_map/ppermute | solution.py:313
  45.1 0.8 %shard_map.95 = (s32[1,128]{1,0:T(1,128)S(1)}, s32[1]{0:T(128)}) custom-call(s32[1]{0:T(128)} %bitcast.5.me_ref, s32[1,128]{1,0:T(1,128)S(1)} %bitcast.38, f32[32,128]{1,0:T(8,128)S(1)} %get-tuple-element.82.count_ref), custom_call_target="tpu_custom_call" | custom-call | bytes 6000000 | tf_op jit(solution)/shard_map/pallas_call | solution.py:23
  45.9 1.8 %shard_map.94.refs_0_ = f32[128,128]{1,0:T(8,128)S(1)} custom-call(s32[1]{0:T(128)} %bitcast.11.side_ref, bf16[8192,128]{1,0:T(8,128)(2,1)S(1)} %copy-done, bf16[128,1024]{1,0:T(8,128)(2,1)} %refs_0_.1, bf16[128,1024]{1,0:T(8,128)(2,1)} %collective-permute-done.refs_1_, bf16[128,1024]{1,0:T(8,128)(2,1)} %collective-permute-done.1.refs_2_, ...), custom_call_target="tpu_custom_call" | custom-call | bytes 3000000 | tf_op jit(solution)/shard_map/pallas_call | solution.py:23
  47.7 4.0 %all-to-all-done.4.parts_ref = bf16[8,144,128]{2,1,0:T(8,128)(2,1)S(1)} async-done(((bf16[8,144,128]{2,1,0:T(8,128)(2,1)}), bf16[8,144,128]{2,1,0:T(8,128)(2,1)S(1)}, u32[]{:S(2)}, u32[]{:S(2)}) %all-to-all-start.4) | async-done | bytes 294944 | tf_op jit(solution)/shard_map/all_to_all | solution.py:257
  51.7 2.3 %shard_map.96 = bf16[512,128]{1,0:T(8,128)(2,1)} custom-call(bf16[8,144,128]{2,1,0:T(8,128)(2,1)S(1)} %all-to-all-done.4.parts_ref, bf16[160,128]{1,0:T(8,128)(2,1)S(1)} %get-tuple-element.88.name_ref, s32[1,512]{1,0:T(1,128)S(1)} %get-tuple-element.89.at_ref, bf16[1024,128]{1,0:T(8,128)(2,1)} %bitcast.34), custom_call_target="tpu_custom_call" | custom-call | bytes 6000000 | tf_op jit(solution)/shard_map/pallas_call | solution.py:23
  54.0 9.9 %all-to-all-start.5 = ((bf16[32,16,128]{2,1,0:T(8,128)(2,1)}), bf16[32,16,128]{2,1,0:T(8,128)(2,1)S(1)}, u32[]{:S(2)}, u32[]{:S(2)}) async-start(bf16[32,16,128]{2,1,0:T(8,128)(2,1)} %bitcast.13), calls=%async_computation.5 | async-start | bytes 262144 | tf_op jit(solution)/shard_map/all_to_all | solution.py:257
  63.9 0.9 %shard_map.98.own_ref = f32[128,128]{1,0:T(8,128)S(1)} custom-call(s32[1,128]{1,0:T(1,128)S(1)} %bitcast.39, s32[1,48]{1,0:T(1,128)S(1)} %copy-done.4, s32[1,32]{1,0:T(1,128)S(1)} %copy-done.5, bf16[8,144,128]{2,1,0:T(8,128)(2,1)S(1)} %all-to-all-done.4.parts_ref, bf16[3072,128]{1,0:T(8,128)(2,1)S(1)} %bitcast.30), custom_call_target="tpu_custom_call" | custom-call | bytes 3000000 | tf_op jit(solution)/shard_map/pallas_call | solution.py:23
  64.8 1.5 %shard_map.97.base_ref = f32[128,128]{1,0:T(8,128)S(1)} custom-call(s32[1]{0:T(128)} %bitcast.11.side_ref, bf16[8192,128]{1,0:T(8,128)(2,1)S(1)} %copy-done, f32[128,128]{1,0:T(8,128)S(1)} %shard_map.94.refs_0_, bf16[128,1024]{1,0:T(8,128)(2,1)} %collective-permute-done.4.refs_1_, bf16[128,1024]{1,0:T(8,128)(2,1)} %collective-permute-done.5.refs_2_, ...), custom_call_target="tpu_custom_call" | custom-call | bytes 3000000 | tf_op jit(solution)/shard_map/pallas_call | solution.py:23
  66.4 5.2 %all-to-all-done.5 = bf16[32,16,128]{2,1,0:T(8,128)(2,1)S(1)} async-done(((bf16[32,16,128]{2,1,0:T(8,128)(2,1)}), bf16[32,16,128]{2,1,0:T(8,128)(2,1)S(1)}, u32[]{:S(2)}, u32[]{:S(2)}) %all-to-all-start.5) | async-done | bytes 131104 | tf_op jit(solution)/shard_map/all_to_all | solution.py:257
  71.6 0.7 %while.12 = (s32[]{:T(128)}, s32[1,128]{1,0:T(1,128)S(1)}, f32[128,128]{1,0:T(8,128)S(1)}, s32[1]{0:T(128)}, s32[1]{0:T(128)}, /*index=5*/s32[1,128]{1,0:T(1,128...) while((s32[]{:T(128)}, s32[1,128]{1,0:T(1,128)S(1)}, ...), condition=%wide.region_1.0_spmd, body=%wide.region_0.0_spmd.sunk | while | flops 2 | bytes 39321952 | solution.py:355
  72.3 1.0 %shard_map.99 = bf16[128,128]{1,0:T(8,128)(2,1)} custom-call(s32[1]{0:T(128)} %bitcast.5.me_ref, s32[1,128]{1,0:T(1,128)S(1)} %get-tuple-element.215, s32[1,128]{1,0:T(1,128)S(1)} %broadcast_in_dim.6.todo_ref, bf16[512,128]{1,0:T(8,128)(2,1)S(1)} %bitcast.31, f32[128,128]{1,0:T(8,128)S(1)} %shard_map.97.base_ref, f32[128,128]{1,0:T(8,128)S(1)} %shard_map.98.own_ref, ...), custom_call_target="tpu_custom_call" | custom-call | bytes 3000000 | tf_op jit(solution)/shard_map/pallas_call | solution.py:23
  (24 shorter events, 0.8 us)
Async XLA Ops:
  2.6 18.1 %copy-start.4 = (s32[1,48]{1,0:T(1,128)S(1)}, s32[1,48]{1,0:T(1,128)}, u32[]{:S(2)}) copy-start(s32[1,48]{1,0:T(1,128)} %slot_ref.3) | copy-start | bytes 580
  2.6 18.1 %copy-start.5 = (s32[1,32]{1,0:T(1,128)S(1)}, s32[1,32]{1,0:T(1,128)}, u32[]{:S(2)}) copy-start(s32[1,32]{1,0:T(1,128)} %evict_ref.3) | copy-start | bytes 388
  2.6 18.1 %copy-start.8 = (s32[128]{0:T(128)S(1)}, s32[128]{0:T(128)}, u32[]{:S(2)}) copy-start(s32[128]{0:T(128)} %param.20) | copy-start | bytes 1540
  2.6 26.4 %all-to-all-start.3 = ((bf16[32,16,1152]{2,1,0:T(8,128)(2,1)}), bf16[32,16,1152]{2,1,0:T(8,128)(2,1)S(1)}, u32[]{:S(2)}, u32[]{:S(2)}) async-start(bf16[32,16,1152]{2,1,0:T(8,128)(2,1)} %bitcast.7), calls=%async_computation.3 | async-start | bytes 2359296 | tf_op jit(solution)/shard_map/all_to_all | solution.py:257
  11.4 21.7 %collective-permute-start = (bf16[128,1024]{1,0:T(8,128)(2,1)}, bf16[128,1024]{1,0:T(8,128)(2,1)}, u32[]{:S(2)}, u32[]{:S(2)}) collective-permute-start(bf16[128,1024]{1,0:T(8,128)(2,1)} %refs_0_.1), channel_id=1, source_target_pairs={{0,1},{1,2},{2,3},{3,4},{4,5},{5,6},{6,7},{7,0},{8,9},{9,10},{10,1... | collective-permute-start | bytes 786440 | tf_op jit(solution)/shard_map/ppermute | solution.py:313
  13.1 20.0 %collective-permute-start.1 = (bf16[128,1024]{1,0:T(8,128)(2,1)}, bf16[128,1024]{1,0:T(8,128)(2,1)}, u32[]{:S(2)}, u32[]{:S(2)}) collective-permute-start(bf16[128,1024]{1,0:T(8,128)(2,1)} %refs_0_.1), channel_id=1, source_target_pairs={{0,7},{1,0},{2,1},{3,2},{4,3},{5,4},{6,5},{7,6},{8,15},{9,8},{10,9... | collective-permute-start | bytes 786440 | tf_op jit(solution)/shard_map/ppermute | solution.py:313
  17.1 15.9 %collective-permute-start.2 = (bf16[128,1024]{1,0:T(8,128)(2,1)}, bf16[128,1024]{1,0:T(8,128)(2,1)}, u32[]{:S(2)}, u32[]{:S(2)}) collective-permute-start(bf16[128,1024]{1,0:T(8,128)(2,1)} %refs_0_.1), channel_id=1, source_target_pairs={{0,2},{1,3},{2,4},{3,5},{4,6},{5,7},{6,0},{7,1},{8,10},{9,11},{10,... | collective-permute-start | bytes 786440 | tf_op jit(solution)/shard_map/ppermute | solution.py:313
  17.1 17.0 %collective-permute-start.3 = (bf16[128,1024]{1,0:T(8,128)(2,1)}, bf16[128,1024]{1,0:T(8,128)(2,1)}, u32[]{:S(2)}, u32[]{:S(2)}) collective-permute-start(bf16[128,1024]{1,0:T(8,128)(2,1)} %refs_0_.1), channel_id=1, source_target_pairs={{0,6},{1,7},{2,0},{3,1},{4,2},{5,3},{6,4},{7,5},{8,14},{9,15},{10,... | collective-permute-start | bytes 786440 | tf_op jit(solution)/shard_map/ppermute | solution.py:313
  20.7 2.8 %copy-start.1 = (bf16[48,64,1024]{2,1,0:T(8,128)(2,1)S(1)}, bf16[48,64,1024]{2,1,0:T(8,128)(2,1)}, u32[]{:S(2)}) copy-start(bf16[48,64,1024]{2,1,0:T(8,128)(2,1)} %param.16) | copy-start | bytes 18874372
  29.0 16.8 %copy-start = (bf16[8192,128]{1,0:T(8,128)(2,1)S(1)}, bf16[8192,128]{1,0:T(8,128)(2,1)}, u32[]{:S(2)}) copy-start(bf16[8192,128]{1,0:T(8,128)(2,1)} %w_ref.3) | copy-start | bytes 6291460
  32.3 0.7 copy-start.3
  34.1 17.6 %all-to-all-start.4 = ((bf16[8,144,128]{2,1,0:T(8,128)(2,1)}), bf16[8,144,128]{2,1,0:T(8,128)(2,1)S(1)}, u32[]{:S(2)}, u32[]{:S(2)}) async-start(bf16[8,144,128]{2,1,0:T(8,128)(2,1)} %copy-done.3), calls=%async_computation.4 | async-start | bytes 589824 | tf_op jit(solution)/shard_map/all_to_all | solution.py:257
  41.3 23.6 %collective-permute-start.4 = (bf16[128,1024]{1,0:T(8,128)(2,1)}, bf16[128,1024]{1,0:T(8,128)(2,1)}, u32[]{:S(2)}, u32[]{:S(2)}) collective-permute-start(bf16[128,1024]{1,0:T(8,128)(2,1)} %collective-permute-done.2.refs_3_), channel_id=1, source_target_pairs={{0,1},{1,2},{2,3},{3,4},{4,5},{5,6},{6,7},{7,0},{8,9},{9,10},{10,1... | collective-permute-start | bytes 786440 | tf_op jit(solution)/shard_map/ppermute | solution.py:313
  42.7 22.1 %collective-permute-start.5 = (bf16[128,1024]{1,0:T(8,128)(2,1)}, bf16[128,1024]{1,0:T(8,128)(2,1)}, u32[]{:S(2)}, u32[]{:S(2)}) collective-permute-start(bf16[128,1024]{1,0:T(8,128)(2,1)} %collective-permute-done.3.refs_4_), channel_id=1, source_target_pairs={{0,7},{1,0},{2,1},{3,2},{4,3},{5,4},{6,5},{7,6},{8,15},{9,8},{10,9... | collective-permute-start | bytes 786440 | tf_op jit(solution)/shard_map/ppermute | solution.py:313
  44.0 20.9 %collective-permute-start.6 = (bf16[128,1024]{1,0:T(8,128)(2,1)}, bf16[128,1024]{1,0:T(8,128)(2,1)}, u32[]{:S(2)}, u32[]{:S(2)}) collective-permute-start(bf16[128,1024]{1,0:T(8,128)(2,1)} %collective-permute-done.2.refs_3_), channel_id=1, source_target_pairs={{0,2},{1,3},{2,4},{3,5},{4,6},{5,7},{6,0},{7,1},{8,10},{9,11},{10,... | collective-permute-start | bytes 786440 | tf_op jit(solution)/shard_map/ppermute | solution.py:313
  47.7 16.3 %copy-start.2 = (bf16[48,64,128]{2,1,0:T(8,128)(2,1)S(1)}, bf16[48,64,128]{2,1,0:T(8,128)(2,1)}, u32[]{:S(2)}) copy-start(bf16[48,64,128]{2,1,0:T(8,128)(2,1)} %param.17) | copy-start | bytes 2359300
  54.0 17.5 %all-to-all-start.5 = ((bf16[32,16,128]{2,1,0:T(8,128)(2,1)}), bf16[32,16,128]{2,1,0:T(8,128)(2,1)S(1)}, u32[]{:S(2)}, u32[]{:S(2)}) async-start(bf16[32,16,128]{2,1,0:T(8,128)(2,1)} %bitcast.13), calls=%async_computation.5 | async-start | bytes 262144 | tf_op jit(solution)/shard_map/all_to_all | solution.py:257
  64.8 6.8 %copy-start.7 = (bf16[16,64,128]{2,1,0:T(8,128)(2,1)S(1)}, bf16[16,64,128]{2,1,0:T(8,128)(2,1)}, u32[]{:S(2)}) copy-start(bf16[16,64,128]{2,1,0:T(8,128)(2,1)} %param.15) | copy-start | bytes 786436

commit v2 on v1

--- a/solution.py
+++ b/solution.py
@@ -37,17 +37,12 @@
     return jnp.sum(jnp.where(down == across, row, 0), axis=1, keepdims=True)
 
 
-def ranks(home, todo):
+def ranks(home, home_at, sent_at):
     n = home.shape[1]
     down = lax.broadcasted_iota(i32, (n, n), 0)
     across = lax.broadcasted_iota(i32, (n, n), 1)
-    before = (column(home) == home) & (column(todo) > 0) & (down < across)
+    before = (home_at == home) & sent_at & (down < across)
     return jnp.sum(before.astype(i32), axis=0, keepdims=True)
-
-
-def targets(home, todo):
-    rank = ranks(home, todo)
-    return jnp.where((todo > 0) & (rank < room), home * room + rank, -1)
 
 
 def dot(a, b):
@@ -58,20 +53,27 @@
     return lax.dot_general(a, b, (((1,), (1,)), ((), ())), preferred_element_type=f32)
 
 
-def pack_kernel(per_home, me_ref, ids_ref, todo_ref, x_ref, out_ref):
+def pack_kernel(per_home, me_ref, ids_ref, *refs):
+    *todo, x_ref, out_ref, to_ref = refs
     slots = out_ref.shape[0]
     width = x_ref.shape[1]
     ids = ids_ref[...]
     n = ids.shape[1]
-    home = ids // per_home
-    todo = jnp.where(home != me_ref[0], todo_ref[...], 0)
-    to = targets(home, todo)
+    ids_at = column(ids)
+    home, home_at = ids // per_home, ids_at // per_home
+    sent, sent_at = home != me_ref[0], home_at != me_ref[0]
+    if todo:
+        sent = sent & (todo[0][...] > 0)
+        sent_at = sent_at & (column(todo[0][...]) > 0)
+    rank = ranks(home, home_at, sent_at)
+    to = jnp.where(sent & (rank < room), home * room + rank, -1)
+    to_ref[...] = to
     place = (lax.broadcasted_iota(i32, (slots, n), 0) == to).astype(bf16)
     out_ref[:, :width] = dot(place, x_ref[...]).astype(bf16)
     lane = lax.broadcasted_iota(i32, (n, lanes), 1)
-    which = (lane == column(ids % per_home)).astype(bf16)
+    which = (lane == ids_at % per_home).astype(bf16)
     tag = dot(place, which)
-    wanted = (lane == column(home) + first_count) & (column(todo) > 0)
+    wanted = (lane == home_at + first_count) & sent_at
     counts = jnp.sum(wanted.astype(f32), axis=0, keepdims=True)
     lane = lax.broadcasted_iota(i32, (slots, lanes), 1)
     out_ref[:, width:] = jnp.where(lane >= first_count, counts, tag).astype(bf16)
@@ -81,7 +83,6 @@
     ids = ids_ref[...]
     home = ids // per_home
     away = home != me_ref[0]
-    todo = away.astype(i32)
     counts = count_ref[...]
     replicas = counts.shape[0]
     sent = jnp.minimum(counts, float(room))
@@ -96,7 +97,8 @@
     mine = jnp.sum(jnp.where(mine, ahead, 0.0), axis=0, keepdims=True).astype(i32)
     at = lax.broadcasted_iota(i32, (lanes, home.shape[1]), 0)
     mine = jnp.sum(jnp.where(at == home + first_count, column(mine), 0), axis=0, keepdims=True)
-    rank = ranks(home, todo)
+    home_at = column(home)
+    rank = ranks(home, home_at, home_at != me_ref[0])
     served = (rank < room) & (mine + rank < fits)
     todo_ref[...] = jnp.where(away & ~served, 1, 0)
 
@@ -232,25 +234,20 @@
     out_ref[...] = sum_
 
 
-def came_back(per_home, me_ref, ids_ref, todo_ref, back_ref):
+def came_back(to_ref, back_ref):
     slots = back_ref.shape[0]
-    home = ids_ref[...] // per_home
-    todo = jnp.where(home != me_ref[0], todo_ref[...], 0)
-    place = (lax.broadcasted_iota(i32, (slots, home.shape[1]), 0) == targets(home, todo)).astype(bf16)
+    place = (lax.broadcasted_iota(i32, (slots, to_ref.shape[1]), 0) == to_ref[...]).astype(bf16)
     return lax.dot_general(place, back_ref[...], (((0,), (0,)), ((), ())), preferred_element_type=f32)
 
 
-def last_kernel(per_home, me_ref, ids_ref, todo_ref, back_ref, base_ref, own_ref, more_ref, out_ref):
-    came = came_back(per_home, me_ref, ids_ref, todo_ref, back_ref)
-    lora = own_ref[...] + more_ref[...] + came
+def last_kernel(to_ref, back_ref, base_ref, own_ref, more_ref, out_ref):
+    lora = own_ref[...] + more_ref[...] + came_back(to_ref, back_ref)
     out_ref[...] = (base_ref[...] + adapter_scale * lora).astype(bf16)
 
 
-def more_kernel(per_home, me_ref, ids_ref, todo_ref, back_ref, more_ref, out_ref, left_ref):
-    out_ref[...] = more_ref[...] + came_back(per_home, me_ref, ids_ref, todo_ref, back_ref)
-    home = ids_ref[...] // per_home
-    todo = todo_ref[...]
-    left_ref[...] = jnp.where(ranks(home, todo) < room, 0, todo)
+def more_kernel(to_ref, todo_ref, back_ref, more_ref, out_ref, left_ref):
+    out_ref[...] = more_ref[...] + came_back(to_ref, back_ref)
+    left_ref[...] = jnp.where(to_ref[...] >= 0, 0, todo_ref[...])
 
 
 def swap(blocks, axis):
@@ -272,14 +269,14 @@
     a_all = home_a.reshape(per_home * inner, width)
     b_all = home_b.reshape(per_home * inner, cols)
 
-    def send(todo):
-        packed = call(
+    def send(*todo):
+        packed, to = call(
             functools.partial(pack_kernel, per_home),
-            jax.ShapeDtypeStruct((slots, width + lanes), bf16),
-            me, ids, todo, x_rows, smem=1, us=3,
+            (jax.ShapeDtypeStruct((slots, width + lanes), bf16), jax.ShapeDtypeStruct((1, n), i32)),
+            me, ids, *todo, x_rows, smem=1, us=3,
         )
         got = swap(packed.reshape(replicas, room, width + lanes), "replica")
-        return got.reshape(slots, width + lanes)
+        return got.reshape(slots, width + lanes), to
 
     def down(got, held, *own):
         rows = held // 2 + sum(o.shape[0] for o in own)
@@ -301,8 +298,7 @@
     def give(back):
         return swap(back.reshape(replicas, room, cols), "replica").reshape(slots, cols)
 
-    todo = jnp.ones((1, n), i32)
-    got = send(todo)
+    got, to = send()
     own = call(
         functools.partial(own_down_kernel, inner),
         jax.ShapeDtypeStruct((n // 2, lanes), bf16),
@@ -342,21 +338,22 @@
 
     def again(state):
         turn, unserved, more = state
-        part, name, at, _ = down(send(unserved), slots)
+        got, to = send(unserved)
+        part, name, at, _ = down(got, slots)
         back = give(up(swap(part, "tensor"), name, at))
         more, unserved = call(
-            functools.partial(more_kernel, per_home),
+            more_kernel,
             (jax.ShapeDtypeStruct((n, cols), f32), jax.ShapeDtypeStruct((1, n), i32)),
-            me, ids, unserved, back, more, smem=1,
+            to, unserved, back, more,
         )
         return turn + 1, unserved, more
 
     state = (jnp.int32(0), unserved, jnp.zeros((n, cols), f32))
     _, _, more = lax.while_loop(lambda s: s[0] < turns[0], again, state)
     return call(
-        functools.partial(last_kernel, per_home),
+        last_kernel,
         jax.ShapeDtypeStruct((n, cols), bf16),
-        me, ids, todo, back, frozen, own_lora, more, smem=1,
+        to, back, frozen, own_lora, more,
     )
 
 

time: 73.9 us -> 73.7 us (level)
  no operation moved by 1% of the time
where the time goes in v2:
time: 73.7 us; the launch traced here: 73.2 us
  starting transfers between devices  38.9 us (53%)
  Pallas kernels  17 us (23%)
  waiting for transfers between devices  12.8 us (17%)
  local copies, waits for them, and re-layouts  3.51 us (5%)
  loops' own time  0.82 us (1%)
    all_to_all x3, starting transfers between devices, swap(): return lax.all_to_all(blocks, axis, split_axis=0, concat_axis=0, tiled=True)  25.8 us
    pallas_call x9, Pallas kernels, call(): pl.pallas_call(kernel, out_shape=out_shape, in_specs=[scalar] * smem + [w...  17 us
    ppermute x7, starting transfers between devices, shift(): lax.ppermute(block, 'tensor', [(k, (k + by) % sides) for k in range(sides)])  13.1 us
    all_to_all x3, waiting for transfers between devices, swap(): return lax.all_to_all(blocks, axis, split_axis=0, concat_axis=0, tiled=True)  11.7 us
    unnamed x16, local copies, waits for them, and re-layouts  3.51 us
  transfers between devices with their start and end apart: 10, of which 4 were waited for; matrix products, arithmetic and copies ran while one was open for 0% of the time, Pallas kernels for 19%

profile of v2, /device:TPU:1, one launch (start us, length us, event | category | flops | bytes accessed | tf_op | source)
XLA Modules:
  0.0 73.2 jit_solution(5625742880554585664)
XLA Ops:
  0.0 2.6 %shard_map.91 = (bf16[512,1152]{1,0:T(8,128)(2,1)}, s32[1,128]{1,0:T(1,128)S(1)}) custom-call(s32[1]{0:T(128)} %bitcast.5.me_ref, s32[1,128]{1,0:T(1,128)} %bitcast.36, bf16[128,1024]{1,0:T(8,128)(2,1)} %refs_0_.3), custom_call_target="tpu_custom_call" | custom-call | bytes 9000000 | tf_op jit(solution)/shard_map/pallas_call | solution.py:23
  2.6 8.7 %all-to-all-start.3 = ((bf16[32,16,1152]{2,1,0:T(8,128)(2,1)}), bf16[32,16,1152]{2,1,0:T(8,128)(2,1)S(1)}, u32[]{:S(2)}, u32[]{:S(2)}) async-start(bf16[32,16,1152]{2,1,0:T(8,128)(2,1)} %bitcast.7), calls=%async_computation.3 | async-start | bytes 2359296 | tf_op jit(solution)/shard_map/all_to_all | solution.py:254
  11.3 1.7 %collective-permute-start = (bf16[128,1024]{1,0:T(8,128)(2,1)}, bf16[128,1024]{1,0:T(8,128)(2,1)}, u32[]{:S(2)}, u32[]{:S(2)}) collective-permute-start(bf16[128,1024]{1,0:T(8,128)(2,1)} %refs_0_.3), channel_id=1, source_target_pairs={{0,1},{1,2},{2,3},{3,4},{4,5},{5,6},{6,7},{7,0},{8,9},{9,10},{10,1... | collective-permute-start | bytes 786440 | tf_op jit(solution)/shard_map/ppermute | solution.py:309
  13.1 4.0 %collective-permute-start.1 = (bf16[128,1024]{1,0:T(8,128)(2,1)}, bf16[128,1024]{1,0:T(8,128)(2,1)}, u32[]{:S(2)}, u32[]{:S(2)}) collective-permute-start(bf16[128,1024]{1,0:T(8,128)(2,1)} %refs_0_.3), channel_id=1, source_target_pairs={{0,7},{1,0},{2,1},{3,2},{4,3},{5,4},{6,5},{7,6},{8,15},{9,8},{10,9... | collective-permute-start | bytes 786440 | tf_op jit(solution)/shard_map/ppermute | solution.py:309
  17.1 3.6 %collective-permute-start.3 = (bf16[128,1024]{1,0:T(8,128)(2,1)}, bf16[128,1024]{1,0:T(8,128)(2,1)}, u32[]{:S(2)}, u32[]{:S(2)}) collective-permute-start(bf16[128,1024]{1,0:T(8,128)(2,1)} %refs_0_.3), channel_id=1, source_target_pairs={{0,6},{1,7},{2,0},{3,1},{4,2},{5,3},{6,4},{7,5},{8,14},{9,15},{10,... | collective-permute-start | bytes 786440 | tf_op jit(solution)/shard_map/ppermute | solution.py:309
  20.7 2.8 %copy-done.1 = bf16[48,64,1024]{2,1,0:T(8,128)(2,1)S(1)} copy-done((bf16[48,64,1024]{2,1,0:T(8,128)(2,1)S(1)}, bf16[48,64,1024]{2,1,0:T(8,128)(2,1)}, u32[]{:S(2)}) %copy-start.1) | copy-done | bytes 6291480
  23.5 3.1 %shard_map.92.refs_0_ = bf16[64,128]{1,0:T(8,128)(2,1)S(1)} custom-call(s32[1,128]{1,0:T(1,128)S(1)} %bitcast.37, s32[1,48]{1,0:T(1,128)S(1)} %copy-done.4, s32[1,32]{1,0:T(1,128)S(1)} %copy-done.5, bf16[128,1024]{1,0:T(8,128)(2,1)} %refs_0_.3, bf16[3072,1024]{1,0:T(8,128)(2,1)S(1)} %bitcast.28), custom_call_target="tpu_custom_call" | custom-call | bytes 9000000 | tf_op jit(solution)/shard_map/pallas_call | solution.py:23
  26.6 2.5 %all-to-all-done.3 = bf16[32,16,1152]{2,1,0:T(8,128)(2,1)S(1)} async-done(((bf16[32,16,1152]{2,1,0:T(8,128)(2,1)}), bf16[32,16,1152]{2,1,0:T(8,128)(2,1)S(1)}, u32[]{:S(2)}, u32[]{:S(2)}) %all-to-all-start.3) | async-done | bytes 1179680 | tf_op jit(solution)/shard_map/all_to_all | solution.py:254
  29.0 3.3 %shard_map.93 = (bf16[8,144,128]{2,1,0:T(8,128)(2,1)S(1)}, bf16[160,128]{1,0:T(8,128)(2,1)S(1)}, s32[1,512]{1,0:T(1,128)S(1)}, f32[32,128]{1,0:T(8,128)S(1)}) custom-call(bf16[512,1152]{1,0:T(8,128)(2,1)S(1)} %bitcast.29, bf16[1024,1024]{1,0:T(8,128)(2,1)} %bitcast.32, bf16[64,128]{1,0:T(8,128)(2,1)S(1)} %shard_map.92.refs_0_), custom_call_target="tpu_custom_call" | custom-call | bytes 9000000 | tf_op jit(solution)/shard_map/pallas_call | solution.py:23
  33.0 1.1 %collective-permute-done.3.refs_4_ = bf16[128,1024]{1,0:T(8,128)(2,1)} collective-permute-done((bf16[128,1024]{1,0:T(8,128)(2,1)}, bf16[128,1024]{1,0:T(8,128)(2,1)}, u32[]{:S(2)}, u32[]{:S(2)}) %collective-permute-start.3) | collective-permute-done | bytes 262176 | tf_op jit(solution)/shard_map/ppermute | solution.py:309
  34.1 7.1 %all-to-all-start.4 = ((bf16[8,144,128]{2,1,0:T(8,128)(2,1)}), bf16[8,144,128]{2,1,0:T(8,128)(2,1)S(1)}, u32[]{:S(2)}, u32[]{:S(2)}) async-start(bf16[8,144,128]{2,1,0:T(8,128)(2,1)} %copy-done.3), calls=%async_computation.4 | async-start | bytes 589824 | tf_op jit(solution)/shard_map/all_to_all | solution.py:254
  41.2 1.5 %collective-permute-start.4 = (bf16[128,1024]{1,0:T(8,128)(2,1)}, bf16[128,1024]{1,0:T(8,128)(2,1)}, u32[]{:S(2)}, u32[]{:S(2)}) collective-permute-start(bf16[128,1024]{1,0:T(8,128)(2,1)} %collective-permute-done.2.refs_3_), channel_id=1, source_target_pairs={{0,1},{1,2},{2,3},{3,4},{4,5},{5,6},{6,7},{7,0},{8,9},{9,10},{10,1... | collective-permute-start | bytes 786440 | tf_op jit(solution)/shard_map/ppermute | solution.py:309
  42.7 1.2 %collective-permute-start.5 = (bf16[128,1024]{1,0:T(8,128)(2,1)}, bf16[128,1024]{1,0:T(8,128)(2,1)}, u32[]{:S(2)}, u32[]{:S(2)}) collective-permute-start(bf16[128,1024]{1,0:T(8,128)(2,1)} %collective-permute-done.3.refs_4_), channel_id=1, source_target_pairs={{0,7},{1,0},{2,1},{3,2},{4,3},{5,4},{6,5},{7,6},{8,15},{9,8},{10,9... | collective-permute-start | bytes 786440 | tf_op jit(solution)/shard_map/ppermute | solution.py:309
  43.9 1.1 %collective-permute-start.6 = (bf16[128,1024]{1,0:T(8,128)(2,1)}, bf16[128,1024]{1,0:T(8,128)(2,1)}, u32[]{:S(2)}, u32[]{:S(2)}) collective-permute-start(bf16[128,1024]{1,0:T(8,128)(2,1)} %collective-permute-done.2.refs_3_), channel_id=1, source_target_pairs={{0,2},{1,3},{2,4},{3,5},{4,6},{5,7},{6,0},{7,1},{8,10},{9,11},{10,... | collective-permute-start | bytes 786440 | tf_op jit(solution)/shard_map/ppermute | solution.py:309
  45.1 0.8 %shard_map.95 = (s32[1,128]{1,0:T(1,128)S(1)}, s32[1]{0:T(128)}) custom-call(s32[1]{0:T(128)} %bitcast.5.me_ref, s32[1,128]{1,0:T(1,128)S(1)} %bitcast.38, f32[32,128]{1,0:T(8,128)S(1)} %get-tuple-element.88.count_ref), custom_call_target="tpu_custom_call" | custom-call | bytes 6000000 | tf_op jit(solution)/shard_map/pallas_call | solution.py:23
  45.8 1.8 %shard_map.94.refs_0_ = f32[128,128]{1,0:T(8,128)S(1)} custom-call(s32[1]{0:T(128)} %bitcast.11.side_ref, bf16[8192,128]{1,0:T(8,128)(2,1)S(1)} %copy-done, bf16[128,1024]{1,0:T(8,128)(2,1)} %refs_0_.3, bf16[128,1024]{1,0:T(8,128)(2,1)} %collective-permute-done.refs_1_, bf16[128,1024]{1,0:T(8,128)(2,1)} %collective-permute-done.1.refs_2_, ...), custom_call_target="tpu_custom_call" | custom-call | bytes 3000000 | tf_op jit(solution)/shard_map/pallas_call | solution.py:23
  47.6 4.0 %all-to-all-done.4.parts_ref = bf16[8,144,128]{2,1,0:T(8,128)(2,1)S(1)} async-done(((bf16[8,144,128]{2,1,0:T(8,128)(2,1)}), bf16[8,144,128]{2,1,0:T(8,128)(2,1)S(1)}, u32[]{:S(2)}, u32[]{:S(2)}) %all-to-all-start.4) | async-done | bytes 294944 | tf_op jit(solution)/shard_map/all_to_all | solution.py:254
  51.7 2.3 %shard_map.96 = bf16[512,128]{1,0:T(8,128)(2,1)} custom-call(bf16[8,144,128]{2,1,0:T(8,128)(2,1)S(1)} %all-to-all-done.4.parts_ref, bf16[160,128]{1,0:T(8,128)(2,1)S(1)} %get-tuple-element.94.name_ref, s32[1,512]{1,0:T(1,128)S(1)} %get-tuple-element.95.at_ref, bf16[1024,128]{1,0:T(8,128)(2,1)} %bitcast.34), custom_call_target="tpu_custom_call" | custom-call | bytes 6000000 | tf_op jit(solution)/shard_map/pallas_call | solution.py:23
  54.0 9.9 %all-to-all-start.5 = ((bf16[32,16,128]{2,1,0:T(8,128)(2,1)}), bf16[32,16,128]{2,1,0:T(8,128)(2,1)S(1)}, u32[]{:S(2)}, u32[]{:S(2)}) async-start(bf16[32,16,128]{2,1,0:T(8,128)(2,1)} %bitcast.13), calls=%async_computation.5 | async-start | bytes 262144 | tf_op jit(solution)/shard_map/all_to_all | solution.py:254
  63.9 0.9 %shard_map.98.own_ref = f32[128,128]{1,0:T(8,128)S(1)} custom-call(s32[1,128]{1,0:T(1,128)S(1)} %bitcast.39, s32[1,48]{1,0:T(1,128)S(1)} %copy-done.4, s32[1,32]{1,0:T(1,128)S(1)} %copy-done.5, bf16[8,144,128]{2,1,0:T(8,128)(2,1)S(1)} %all-to-all-done.4.parts_ref, bf16[3072,128]{1,0:T(8,128)(2,1)S(1)} %bitcast.30), custom_call_target="tpu_custom_call" | custom-call | bytes 3000000 | tf_op jit(solution)/shard_map/pallas_call | solution.py:23
  64.8 1.5 %shard_map.97.base_ref = f32[128,128]{1,0:T(8,128)S(1)} custom-call(s32[1]{0:T(128)} %bitcast.11.side_ref, bf16[8192,128]{1,0:T(8,128)(2,1)S(1)} %copy-done, f32[128,128]{1,0:T(8,128)S(1)} %shard_map.94.refs_0_, bf16[128,1024]{1,0:T(8,128)(2,1)} %collective-permute-done.4.refs_1_, bf16[128,1024]{1,0:T(8,128)(2,1)} %collective-permute-done.5.refs_2_, ...), custom_call_target="tpu_custom_call" | custom-call | bytes 3000000 | tf_op jit(solution)/shard_map/pallas_call | solution.py:23
  66.3 5.2 %all-to-all-done.5 = bf16[32,16,128]{2,1,0:T(8,128)(2,1)S(1)} async-done(((bf16[32,16,128]{2,1,0:T(8,128)(2,1)}), bf16[32,16,128]{2,1,0:T(8,128)(2,1)S(1)}, u32[]{:S(2)}, u32[]{:S(2)}) %all-to-all-start.5) | async-done | bytes 131104 | tf_op jit(solution)/shard_map/all_to_all | solution.py:254
  71.5 0.8 %while.12 = (s32[]{:T(128)}, s32[1,128]{1,0:T(1,128)S(1)}, f32[128,128]{1,0:T(8,128)S(1)}, s32[1]{0:T(128)}, s32[1]{0:T(128)}, /*index=5*/s32[1,128]{1,0:T(1,128...) while((s32[]{:T(128)}, s32[1,128]{1,0:T(1,128)S(1)}, ...), condition=%wide.region_1.0_spmd, body=%wide.region_0.0_spmd.sunk | while | flops 2 | bytes 39321952 | solution.py:352
  72.4 0.9 %shard_map.99 = bf16[128,128]{1,0:T(8,128)(2,1)} custom-call(s32[1,128]{1,0:T(1,128)S(1)} %get-tuple-element.80.to_ref, bf16[512,128]{1,0:T(8,128)(2,1)S(1)} %bitcast.31, f32[128,128]{1,0:T(8,128)S(1)} %shard_map.97.base_ref, f32[128,128]{1,0:T(8,128)S(1)} %shard_map.98.own_ref, f32[128,128]{1,0:T(8,128)S(1)} %get-tuple-element.100.more_ref), custom_call_target="tpu_custom_call" | custom-call | bytes 3000000 | tf_op jit(solution)/shard_map/pallas_call | solution.py:23
  (23 shorter events, 0.8 us)
Async XLA Ops:
  2.6 18.1 %copy-start.4 = (s32[1,48]{1,0:T(1,128)S(1)}, s32[1,48]{1,0:T(1,128)}, u32[]{:S(2)}) copy-start(s32[1,48]{1,0:T(1,128)} %slot_ref.3) | copy-start | bytes 580
  2.6 18.1 %copy-start.5 = (s32[1,32]{1,0:T(1,128)S(1)}, s32[1,32]{1,0:T(1,128)}, u32[]{:S(2)}) copy-start(s32[1,32]{1,0:T(1,128)} %evict_ref.3) | copy-start | bytes 388
  2.6 18.1 %copy-start.8 = (s32[128]{0:T(128)S(1)}, s32[128]{0:T(128)}, u32[]{:S(2)}) copy-start(s32[128]{0:T(128)} %param.20) | copy-start | bytes 1540
  2.6 26.4 %all-to-all-start.3 = ((bf16[32,16,1152]{2,1,0:T(8,128)(2,1)}), bf16[32,16,1152]{2,1,0:T(8,128)(2,1)S(1)}, u32[]{:S(2)}, u32[]{:S(2)}) async-start(bf16[32,16,1152]{2,1,0:T(8,128)(2,1)} %bitcast.7), calls=%async_computation.3 | async-start | bytes 2359296 | tf_op jit(solution)/shard_map/all_to_all | solution.py:254
  11.3 21.7 %collective-permute-start = (bf16[128,1024]{1,0:T(8,128)(2,1)}, bf16[128,1024]{1,0:T(8,128)(2,1)}, u32[]{:S(2)}, u32[]{:S(2)}) collective-permute-start(bf16[128,1024]{1,0:T(8,128)(2,1)} %refs_0_.3), channel_id=1, source_target_pairs={{0,1},{1,2},{2,3},{3,4},{4,5},{5,6},{6,7},{7,0},{8,9},{9,10},{10,1... | collective-permute-start | bytes 786440 | tf_op jit(solution)/shard_map/ppermute | solution.py:309
  13.1 20.0 %collective-permute-start.1 = (bf16[128,1024]{1,0:T(8,128)(2,1)}, bf16[128,1024]{1,0:T(8,128)(2,1)}, u32[]{:S(2)}, u32[]{:S(2)}) collective-permute-start(bf16[128,1024]{1,0:T(8,128)(2,1)} %refs_0_.3), channel_id=1, source_target_pairs={{0,7},{1,0},{2,1},{3,2},{4,3},{5,4},{6,5},{7,6},{8,15},{9,8},{10,9... | collective-permute-start | bytes 786440 | tf_op jit(solution)/shard_map/ppermute | solution.py:309
  17.1 15.9 %collective-permute-start.2 = (bf16[128,1024]{1,0:T(8,128)(2,1)}, bf16[128,1024]{1,0:T(8,128)(2,1)}, u32[]{:S(2)}, u32[]{:S(2)}) collective-permute-start(bf16[128,1024]{1,0:T(8,128)(2,1)} %refs_0_.3), channel_id=1, source_target_pairs={{0,2},{1,3},{2,4},{3,5},{4,6},{5,7},{6,0},{7,1},{8,10},{9,11},{10,... | collective-permute-start | bytes 786440 | tf_op jit(solution)/shard_map/ppermute | solution.py:309
  17.1 17.0 %collective-permute-start.3 = (bf16[128,1024]{1,0:T(8,128)(2,1)}, bf16[128,1024]{1,0:T(8,128)(2,1)}, u32[]{:S(2)}, u32[]{:S(2)}) collective-permute-start(bf16[128,1024]{1,0:T(8,128)(2,1)} %refs_0_.3), channel_id=1, source_target_pairs={{0,6},{1,7},{2,0},{3,1},{4,2},{5,3},{6,4},{7,5},{8,14},{9,15},{10,... | collective-permute-start | bytes 786440 | tf_op jit(solution)/shard_map/ppermute | solution.py:309
  20.7 2.8 %copy-start.1 = (bf16[48,64,1024]{2,1,0:T(8,128)(2,1)S(1)}, bf16[48,64,1024]{2,1,0:T(8,128)(2,1)}, u32[]{:S(2)}) copy-start(bf16[48,64,1024]{2,1,0:T(8,128)(2,1)} %param.16) | copy-start | bytes 18874372
  29.0 16.8 %copy-start = (bf16[8192,128]{1,0:T(8,128)(2,1)S(1)}, bf16[8192,128]{1,0:T(8,128)(2,1)}, u32[]{:S(2)}) copy-start(bf16[8192,128]{1,0:T(8,128)(2,1)} %w_ref.3) | copy-start | bytes 6291460
  32.3 0.7 copy-start.3
  34.1 17.5 %all-to-all-start.4 = ((bf16[8,144,128]{2,1,0:T(8,128)(2,1)}), bf16[8,144,128]{2,1,0:T(8,128)(2,1)S(1)}, u32[]{:S(2)}, u32[]{:S(2)}) async-start(bf16[8,144,128]{2,1,0:T(8,128)(2,1)} %copy-done.3), calls=%async_computation.4 | async-start | bytes 589824 | tf_op jit(solution)/shard_map/all_to_all | solution.py:254
  41.2 23.6 %collective-permute-start.4 = (bf16[128,1024]{1,0:T(8,128)(2,1)}, bf16[128,1024]{1,0:T(8,128)(2,1)}, u32[]{:S(2)}, u32[]{:S(2)}) collective-permute-start(bf16[128,1024]{1,0:T(8,128)(2,1)} %collective-permute-done.2.refs_3_), channel_id=1, source_target_pairs={{0,1},{1,2},{2,3},{3,4},{4,5},{5,6},{6,7},{7,0},{8,9},{9,10},{10,1... | collective-permute-start | bytes 786440 | tf_op jit(solution)/shard_map/ppermute | solution.py:309
  42.7 22.1 %collective-permute-start.5 = (bf16[128,1024]{1,0:T(8,128)(2,1)}, bf16[128,1024]{1,0:T(8,128)(2,1)}, u32[]{:S(2)}, u32[]{:S(2)}) collective-permute-start(bf16[128,1024]{1,0:T(8,128)(2,1)} %collective-permute-done.3.refs_4_), channel_id=1, source_target_pairs={{0,7},{1,0},{2,1},{3,2},{4,3},{5,4},{6,5},{7,6},{8,15},{9,8},{10,9... | collective-permute-start | bytes 786440 | tf_op jit(solution)/shard_map/ppermute | solution.py:309
  43.9 20.9 %collective-permute-start.6 = (bf16[128,1024]{1,0:T(8,128)(2,1)}, bf16[128,1024]{1,0:T(8,128)(2,1)}, u32[]{:S(2)}, u32[]{:S(2)}) collective-permute-start(bf16[128,1024]{1,0:T(8,128)(2,1)} %collective-permute-done.2.refs_3_), channel_id=1, source_target_pairs={{0,2},{1,3},{2,4},{3,5},{4,6},{5,7},{6,0},{7,1},{8,10},{9,11},{10,... | collective-permute-start | bytes 786440 | tf_op jit(solution)/shard_map/ppermute | solution.py:309
  47.6 16.3 %copy-start.2 = (bf16[48,64,128]{2,1,0:T(8,128)(2,1)S(1)}, bf16[48,64,128]{2,1,0:T(8,128)(2,1)}, u32[]{:S(2)}) copy-start(bf16[48,64,128]{2,1,0:T(8,128)(2,1)} %param.17) | copy-start | bytes 2359300
  54.0 17.6 %all-to-all-start.5 = ((bf16[32,16,128]{2,1,0:T(8,128)(2,1)}), bf16[32,16,128]{2,1,0:T(8,128)(2,1)S(1)}, u32[]{:S(2)}, u32[]{:S(2)}) async-start(bf16[32,16,128]{2,1,0:T(8,128)(2,1)} %bitcast.13), calls=%async_computation.5 | async-start | bytes 262144 | tf_op jit(solution)/shard_map/all_to_all | solution.py:254
  64.8 6.8 %copy-start.7 = (bf16[16,64,128]{2,1,0:T(8,128)(2,1)S(1)}, bf16[16,64,128]{2,1,0:T(8,128)(2,1)}, u32[]{:S(2)}) copy-start(bf16[16,64,128]{2,1,0:T(8,128)(2,1)} %param.15) | copy-start | bytes 786436

commit v3 on v2

--- a/solution.py
+++ b/solution.py
@@ -15,16 +15,18 @@
 bf16, f32, i32 = jnp.bfloat16, jnp.float32, jnp.int32
 
 
-def call(kernel, out_shape, *args, smem=0, smem_out=0, us=1, limit=8 << 20):
+def call(kernel, out_shape, *args, smem=0, smem_out=0, hbm_out=0, scratch=(), us=1, limit=8 << 20):
     scalar, whole = pl.BlockSpec(memory_space=pltpu.SMEM), pl.BlockSpec(memory_space=pltpu.VMEM)
     several = isinstance(out_shape, tuple)
     results = len(out_shape) if several else 1
-    out_specs = (whole,) * (results - smem_out) + (scalar,) * smem_out
+    out_specs = (pl.BlockSpec(memory_space=pltpu.HBM),) * hbm_out
+    out_specs += (whole,) * (results - smem_out - hbm_out) + (scalar,) * smem_out
     return pl.pallas_call(
         kernel,
         out_shape=out_shape,
         in_specs=[scalar] * smem + [whole] * (len(args) - smem),
         out_specs=out_specs if several else out_specs[0],
+        scratch_shapes=scratch,
         compiler_params=pltpu.CompilerParams(vmem_limit_bytes=limit),
         cost_estimate=pl.CostEstimate(flops=0, bytes_accessed=us * 3_000_000, transcendentals=0),
     )(*args)
@@ -171,8 +173,8 @@
 
 
 def down_kernel(inner, per_home, got_ref, a_ref, *refs):
-    own_ref = refs[0] if len(refs) == 5 else None
-    out_ref, name_ref, at_ref, count_ref = refs[-4:]
+    own_ref = refs[0] if len(refs) == 7 else None
+    out_ref, name_ref, at_ref, count_ref, part_ref, part_sem = refs[-6:]
     slots = got_ref.shape[0]
     width = a_ref.shape[1]
     held = name_ref.shape[0]
@@ -189,13 +191,19 @@
     lane = lax.broadcasted_iota(i32, (held, lanes), 1)
     name = jnp.where(lane < per_home, name, 0.0).astype(bf16)
     name_ref[...] = name
-    part = fold(masked_down(x, picker(name, inner), a_ref, inner), inner).astype(bf16)
-    for side in range(out_ref.shape[0]):
-        out_ref[side, : held // 2, :] = part
-        if own_ref is not None:
-            out_ref[side, held // 2 :, :] = own_ref[...]
+    part_ref[: held // 2, :] = fold(masked_down(x, picker(name, inner), a_ref, inner), inner).astype(bf16)
+    if own_ref is not None:
+        part_ref[held // 2 :, :] = own_ref[...]
+    copies = [
+        pltpu.make_async_copy(part_ref, out_ref.at[side], part_sem.at[side])
+        for side in range(out_ref.shape[0])
+    ]
+    for copy in copies:
+        copy.start()
     for r in range(count_ref.shape[0]):
         count_ref[r : r + 1, :] = got_ref[r * room : r * room + 1, width:].astype(f32)
+    for copy in copies:
+        copy.wait()
 
 
 def low_of(parts_ref, lo, hi, inner):
@@ -286,7 +294,10 @@
             jax.ShapeDtypeStruct((1, slots), i32),
             jax.ShapeDtypeStruct((replicas, lanes), f32),
         )
-        return call(functools.partial(down_kernel, inner, per_home), out, got, a_all, *own, us=3)
+        return call(
+            functools.partial(down_kernel, inner, per_home), out, got, a_all, *own, us=3, hbm_out=1,
+            scratch=[pltpu.VMEM((rows, lanes), bf16), pltpu.SemaphoreType.DMA((sides,))],
+        )
 
     def up(parts, name, at):
         return call(

time: 73.7 us -> 73.7 us (level)
  no operation moved by 1% of the time
where the time goes in v3:
time: 73.7 us; the launch traced here: 73.2 us
  starting transfers between devices  38.9 us (53%)
  Pallas kernels  17.5 us (24%)
  waiting for transfers between devices  12.3 us (17%)
  local copies, waits for them, and re-layouts  3.51 us (5%)
  loops' own time  0.82 us (1%)
    all_to_all x3, starting transfers between devices, swap(): return lax.all_to_all(blocks, axis, split_axis=0, concat_axis=0, tiled=True)  25.8 us
    pallas_call x9, Pallas kernels, call(): pl.pallas_call(kernel, out_shape=out_shape, in_specs=[scalar] * smem + [w...  17.5 us
    ppermute x7, starting transfers between devices, shift(): lax.ppermute(block, 'tensor', [(k, (k + by) % sides) for k in range(sides)])  13.1 us
    all_to_all x3, waiting for transfers between devices, swap(): return lax.all_to_all(blocks, axis, split_axis=0, concat_axis=0, tiled=True)  11.7 us
    unnamed x16, local copies, waits for them, and re-layouts  3.51 us
  transfers between devices with their start and end apart: 10, of which 4 were waited for; matrix products, arithmetic and copies ran while one was open for 0% of the time, Pallas kernels for 19%

profile of v3, /device:TPU:1, one launch (start us, length us, event | category | flops | bytes accessed | tf_op | source)
XLA Modules:
  0.0 73.2 jit_solution(18234807098938076321)
XLA Ops:
  0.0 2.6 %shard_map.91 = (bf16[512,1152]{1,0:T(8,128)(2,1)}, s32[1,128]{1,0:T(1,128)S(1)}) custom-call(s32[1]{0:T(128)} %bitcast.5.me_ref, s32[1,128]{1,0:T(1,128)} %bitcast.36, bf16[128,1024]{1,0:T(8,128)(2,1)} %refs_0_.3), custom_call_target="tpu_custom_call" | custom-call | bytes 9000000 | tf_op jit(solution)/shard_map/pallas_call | solution.py:24
  2.6 8.7 %all-to-all-start.3 = ((bf16[32,16,1152]{2,1,0:T(8,128)(2,1)}), bf16[32,16,1152]{2,1,0:T(8,128)(2,1)S(1)}, u32[]{:S(2)}, u32[]{:S(2)}) async-start(bf16[32,16,1152]{2,1,0:T(8,128)(2,1)} %bitcast.7), calls=%async_computation.3 | async-start | bytes 2359296 | tf_op jit(solution)/shard_map/all_to_all | solution.py:262
  11.3 1.7 %collective-permute-start = (bf16[128,1024]{1,0:T(8,128)(2,1)}, bf16[128,1024]{1,0:T(8,128)(2,1)}, u32[]{:S(2)}, u32[]{:S(2)}) collective-permute-start(bf16[128,1024]{1,0:T(8,128)(2,1)} %refs_0_.3), channel_id=1, source_target_pairs={{0,1},{1,2},{2,3},{3,4},{4,5},{5,6},{6,7},{7,0},{8,9},{9,10},{10,1... | collective-permute-start | bytes 786440 | tf_op jit(solution)/shard_map/ppermute | solution.py:320
  13.1 4.0 %collective-permute-start.1 = (bf16[128,1024]{1,0:T(8,128)(2,1)}, bf16[128,1024]{1,0:T(8,128)(2,1)}, u32[]{:S(2)}, u32[]{:S(2)}) collective-permute-start(bf16[128,1024]{1,0:T(8,128)(2,1)} %refs_0_.3), channel_id=1, source_target_pairs={{0,7},{1,0},{2,1},{3,2},{4,3},{5,4},{6,5},{7,6},{8,15},{9,8},{10,9... | collective-permute-start | bytes 786440 | tf_op jit(solution)/shard_map/ppermute | solution.py:320
  17.1 3.6 %collective-permute-start.3 = (bf16[128,1024]{1,0:T(8,128)(2,1)}, bf16[128,1024]{1,0:T(8,128)(2,1)}, u32[]{:S(2)}, u32[]{:S(2)}) collective-permute-start(bf16[128,1024]{1,0:T(8,128)(2,1)} %refs_0_.3), channel_id=1, source_target_pairs={{0,6},{1,7},{2,0},{3,1},{4,2},{5,3},{6,4},{7,5},{8,14},{9,15},{10,... | collective-permute-start | bytes 786440 | tf_op jit(solution)/shard_map/ppermute | solution.py:320
  20.7 2.8 %copy-done.1 = bf16[48,64,1024]{2,1,0:T(8,128)(2,1)S(1)} copy-done((bf16[48,64,1024]{2,1,0:T(8,128)(2,1)S(1)}, bf16[48,64,1024]{2,1,0:T(8,128)(2,1)}, u32[]{:S(2)}) %copy-start.1) | copy-done | bytes 6291480
  23.5 3.1 %shard_map.92.refs_0_ = bf16[64,128]{1,0:T(8,128)(2,1)S(1)} custom-call(s32[1,128]{1,0:T(1,128)S(1)} %bitcast.37, s32[1,48]{1,0:T(1,128)S(1)} %copy-done.4, s32[1,32]{1,0:T(1,128)S(1)} %copy-done.5, bf16[128,1024]{1,0:T(8,128)(2,1)} %refs_0_.3, bf16[3072,1024]{1,0:T(8,128)(2,1)S(1)} %bitcast.28), custom_call_target="tpu_custom_call" | custom-call | bytes 9000000 | tf_op jit(solution)/shard_map/pallas_call | solution.py:24
  26.6 2.5 %all-to-all-done.3 = bf16[32,16,1152]{2,1,0:T(8,128)(2,1)S(1)} async-done(((bf16[32,16,1152]{2,1,0:T(8,128)(2,1)}), bf16[32,16,1152]{2,1,0:T(8,128)(2,1)S(1)}, u32[]{:S(2)}, u32[]{:S(2)}) %all-to-all-start.3) | async-done | bytes 1179680 | tf_op jit(solution)/shard_map/all_to_all | solution.py:262
  29.0 3.7 %shard_map.93 = (bf16[8,144,128]{2,1,0:T(8,128)(2,1)S(1)}, bf16[160,128]{1,0:T(8,128)(2,1)S(1)}, s32[1,512]{1,0:T(1,128)S(1)}, f32[32,128]{1,0:T(8,128)S(1)}) custom-call(bf16[512,1152]{1,0:T(8,128)(2,1)S(1)} %bitcast.29, bf16[1024,1024]{1,0:T(8,128)(2,1)} %bitcast.32, bf16[64,128]{1,0:T(8,128)(2,1)S(1)} %shard_map.92.refs_0_), custom_call_target="tpu_custom_call" | custom-call | bytes 9000000 | tf_op jit(solution)/shard_map/pallas_call | solution.py:24
  32.8 0.7 copy-done.3
  34.1 7.6 %all-to-all-start.4 = ((bf16[8,144,128]{2,1,0:T(8,128)(2,1)}), bf16[8,144,128]{2,1,0:T(8,128)(2,1)S(1)}, u32[]{:S(2)}, u32[]{:S(2)}) async-start(bf16[8,144,128]{2,1,0:T(8,128)(2,1)} %copy-done.3), calls=%async_computation.4 | async-start | bytes 589824 | tf_op jit(solution)/shard_map/all_to_all | solution.py:262
  41.7 1.5 %collective-permute-start.4 = (bf16[128,1024]{1,0:T(8,128)(2,1)}, bf16[128,1024]{1,0:T(8,128)(2,1)}, u32[]{:S(2)}, u32[]{:S(2)}) collective-permute-start(bf16[128,1024]{1,0:T(8,128)(2,1)} %collective-permute-done.2.refs_3_), channel_id=1, source_target_pairs={{0,1},{1,2},{2,3},{3,4},{4,5},{5,6},{6,7},{7,0},{8,9},{9,10},{10,1... | collective-permute-start | bytes 786440 | tf_op jit(solution)/shard_map/ppermute | solution.py:320
  43.1 1.2 %collective-permute-start.5 = (bf16[128,1024]{1,0:T(8,128)(2,1)}, bf16[128,1024]{1,0:T(8,128)(2,1)}, u32[]{:S(2)}, u32[]{:S(2)}) collective-permute-start(bf16[128,1024]{1,0:T(8,128)(2,1)} %collective-permute-done.3.refs_4_), channel_id=1, source_target_pairs={{0,7},{1,0},{2,1},{3,2},{4,3},{5,4},{6,5},{7,6},{8,15},{9,8},{10,9... | collective-permute-start | bytes 786440 | tf_op jit(solution)/shard_map/ppermute | solution.py:320
  44.4 1.1 %collective-permute-start.6 = (bf16[128,1024]{1,0:T(8,128)(2,1)}, bf16[128,1024]{1,0:T(8,128)(2,1)}, u32[]{:S(2)}, u32[]{:S(2)}) collective-permute-start(bf16[128,1024]{1,0:T(8,128)(2,1)} %collective-permute-done.2.refs_3_), channel_id=1, source_target_pairs={{0,2},{1,3},{2,4},{3,5},{4,6},{5,7},{6,0},{7,1},{8,10},{9,11},{10,... | collective-permute-start | bytes 786440 | tf_op jit(solution)/shard_map/ppermute | solution.py:320
  45.5 0.8 %shard_map.95 = (s32[1,128]{1,0:T(1,128)S(1)}, s32[1]{0:T(128)}) custom-call(s32[1]{0:T(128)} %bitcast.5.me_ref, s32[1,128]{1,0:T(1,128)S(1)} %bitcast.38, f32[32,128]{1,0:T(8,128)S(1)} %get-tuple-element.88.count_ref), custom_call_target="tpu_custom_call" | custom-call | bytes 6000000 | tf_op jit(solution)/shard_map/pallas_call | solution.py:24
  46.3 1.8 %shard_map.94.refs_0_ = f32[128,128]{1,0:T(8,128)S(1)} custom-call(s32[1]{0:T(128)} %bitcast.11.side_ref, bf16[8192,128]{1,0:T(8,128)(2,1)S(1)} %copy-done, bf16[128,1024]{1,0:T(8,128)(2,1)} %refs_0_.3, bf16[128,1024]{1,0:T(8,128)(2,1)} %collective-permute-done.refs_1_, bf16[128,1024]{1,0:T(8,128)(2,1)} %collective-permute-done.1.refs_2_, ...), custom_call_target="tpu_custom_call" | custom-call | bytes 3000000 | tf_op jit(solution)/shard_map/pallas_call | solution.py:24
  48.1 4.0 %all-to-all-done.4.parts_ref = bf16[8,144,128]{2,1,0:T(8,128)(2,1)S(1)} async-done(((bf16[8,144,128]{2,1,0:T(8,128)(2,1)}), bf16[8,144,128]{2,1,0:T(8,128)(2,1)S(1)}, u32[]{:S(2)}, u32[]{:S(2)}) %all-to-all-start.4) | async-done | bytes 294944 | tf_op jit(solution)/shard_map/all_to_all | solution.py:262
  52.1 2.3 %shard_map.96 = bf16[512,128]{1,0:T(8,128)(2,1)} custom-call(bf16[8,144,128]{2,1,0:T(8,128)(2,1)S(1)} %all-to-all-done.4.parts_ref, bf16[160,128]{1,0:T(8,128)(2,1)S(1)} %get-tuple-element.94.name_ref, s32[1,512]{1,0:T(1,128)S(1)} %get-tuple-element.95.at_ref, bf16[1024,128]{1,0:T(8,128)(2,1)} %bitcast.34), custom_call_target="tpu_custom_call" | custom-call | bytes 6000000 | tf_op jit(solution)/shard_map/pallas_call | solution.py:24
  54.4 9.5 %all-to-all-start.5 = ((bf16[32,16,128]{2,1,0:T(8,128)(2,1)}), bf16[32,16,128]{2,1,0:T(8,128)(2,1)S(1)}, u32[]{:S(2)}, u32[]{:S(2)}) async-start(bf16[32,16,128]{2,1,0:T(8,128)(2,1)} %bitcast.13), calls=%async_computation.5 | async-start | bytes 262144 | tf_op jit(solution)/shard_map/all_to_all | solution.py:262
  63.9 0.9 %shard_map.98.own_ref = f32[128,128]{1,0:T(8,128)S(1)} custom-call(s32[1,128]{1,0:T(1,128)S(1)} %bitcast.39, s32[1,48]{1,0:T(1,128)S(1)} %copy-done.4, s32[1,32]{1,0:T(1,128)S(1)} %copy-done.5, bf16[8,144,128]{2,1,0:T(8,128)(2,1)S(1)} %all-to-all-done.4.parts_ref, bf16[3072,128]{1,0:T(8,128)(2,1)S(1)} %bitcast.30), custom_call_target="tpu_custom_call" | custom-call | bytes 3000000 | tf_op jit(solution)/shard_map/pallas_call | solution.py:24
  64.8 1.5 %shard_map.97.base_ref = f32[128,128]{1,0:T(8,128)S(1)} custom-call(s32[1]{0:T(128)} %bitcast.11.side_ref, bf16[8192,128]{1,0:T(8,128)(2,1)S(1)} %copy-done, f32[128,128]{1,0:T(8,128)S(1)} %shard_map.94.refs_0_, bf16[128,1024]{1,0:T(8,128)(2,1)} %collective-permute-done.4.refs_1_, bf16[128,1024]{1,0:T(8,128)(2,1)} %collective-permute-done.5.refs_2_, ...), custom_call_target="tpu_custom_call" | custom-call | bytes 3000000 | tf_op jit(solution)/shard_map/pallas_call | solution.py:24
  66.3 5.2 %all-to-all-done.5 = bf16[32,16,128]{2,1,0:T(8,128)(2,1)S(1)} async-done(((bf16[32,16,128]{2,1,0:T(8,128)(2,1)}), bf16[32,16,128]{2,1,0:T(8,128)(2,1)S(1)}, u32[]{:S(2)}, u32[]{:S(2)}) %all-to-all-start.5) | async-done | bytes 131104 | tf_op jit(solution)/shard_map/all_to_all | solution.py:262
  71.5 0.8 %while.12 = (s32[]{:T(128)}, s32[1,128]{1,0:T(1,128)S(1)}, f32[128,128]{1,0:T(8,128)S(1)}, s32[1]{0:T(128)}, s32[1]{0:T(128)}, /*index=5*/s32[1,128]{1,0:T(1,128...) while((s32[]{:T(128)}, s32[1,128]{1,0:T(1,128)S(1)}, ...), condition=%wide.region_1.0_spmd, body=%wide.region_0.0_spmd.sunk | while | flops 2 | bytes 39321952 | solution.py:363
  72.4 0.9 %shard_map.99 = bf16[128,128]{1,0:T(8,128)(2,1)} custom-call(s32[1,128]{1,0:T(1,128)S(1)} %get-tuple-element.80.to_ref, bf16[512,128]{1,0:T(8,128)(2,1)S(1)} %bitcast.31, f32[128,128]{1,0:T(8,128)S(1)} %shard_map.97.base_ref, f32[128,128]{1,0:T(8,128)S(1)} %shard_map.98.own_ref, f32[128,128]{1,0:T(8,128)S(1)} %get-tuple-element.100.more_ref), custom_call_target="tpu_custom_call" | custom-call | bytes 3000000 | tf_op jit(solution)/shard_map/pallas_call | solution.py:24
  (23 shorter events, 0.7 us)
Async XLA Ops:
  2.6 18.1 %copy-start.4 = (s32[1,48]{1,0:T(1,128)S(1)}, s32[1,48]{1,0:T(1,128)}, u32[]{:S(2)}) copy-start(s32[1,48]{1,0:T(1,128)} %slot_ref.3) | copy-start | bytes 580
  2.6 18.1 %copy-start.5 = (s32[1,32]{1,0:T(1,128)S(1)}, s32[1,32]{1,0:T(1,128)}, u32[]{:S(2)}) copy-start(s32[1,32]{1,0:T(1,128)} %evict_ref.3) | copy-start | bytes 388
  2.6 18.1 %copy-start.8 = (s32[128]{0:T(128)S(1)}, s32[128]{0:T(128)}, u32[]{:S(2)}) copy-start(s32[128]{0:T(128)} %param.20) | copy-start | bytes 1540
  2.6 26.4 %all-to-all-start.3 = ((bf16[32,16,1152]{2,1,0:T(8,128)(2,1)}), bf16[32,16,1152]{2,1,0:T(8,128)(2,1)S(1)}, u32[]{:S(2)}, u32[]{:S(2)}) async-start(bf16[32,16,1152]{2,1,0:T(8,128)(2,1)} %bitcast.7), calls=%async_computation.3 | async-start | bytes 2359296 | tf_op jit(solution)/shard_map/all_to_all | solution.py:262
  11.3 22.1 %collective-permute-start = (bf16[128,1024]{1,0:T(8,128)(2,1)}, bf16[128,1024]{1,0:T(8,128)(2,1)}, u32[]{:S(2)}, u32[]{:S(2)}) collective-permute-start(bf16[128,1024]{1,0:T(8,128)(2,1)} %refs_0_.3), channel_id=1, source_target_pairs={{0,1},{1,2},{2,3},{3,4},{4,5},{5,6},{6,7},{7,0},{8,9},{9,10},{10,1... | collective-permute-start | bytes 786440 | tf_op jit(solution)/shard_map/ppermute | solution.py:320
  13.1 20.4 %collective-permute-start.1 = (bf16[128,1024]{1,0:T(8,128)(2,1)}, bf16[128,1024]{1,0:T(8,128)(2,1)}, u32[]{:S(2)}, u32[]{:S(2)}) collective-permute-start(bf16[128,1024]{1,0:T(8,128)(2,1)} %refs_0_.3), channel_id=1, source_target_pairs={{0,7},{1,0},{2,1},{3,2},{4,3},{5,4},{6,5},{7,6},{8,15},{9,8},{10,9... | collective-permute-start | bytes 786440 | tf_op jit(solution)/shard_map/ppermute | solution.py:320
  17.1 16.4 %collective-permute-start.2 = (bf16[128,1024]{1,0:T(8,128)(2,1)}, bf16[128,1024]{1,0:T(8,128)(2,1)}, u32[]{:S(2)}, u32[]{:S(2)}) collective-permute-start(bf16[128,1024]{1,0:T(8,128)(2,1)} %refs_0_.3), channel_id=1, source_target_pairs={{0,2},{1,3},{2,4},{3,5},{4,6},{5,7},{6,0},{7,1},{8,10},{9,11},{10,... | collective-permute-start | bytes 786440 | tf_op jit(solution)/shard_map/ppermute | solution.py:320
  17.1 17.0 %collective-permute-start.3 = (bf16[128,1024]{1,0:T(8,128)(2,1)}, bf16[128,1024]{1,0:T(8,128)(2,1)}, u32[]{:S(2)}, u32[]{:S(2)}) collective-permute-start(bf16[128,1024]{1,0:T(8,128)(2,1)} %refs_0_.3), channel_id=1, source_target_pairs={{0,6},{1,7},{2,0},{3,1},{4,2},{5,3},{6,4},{7,5},{8,14},{9,15},{10,... | collective-permute-start | bytes 786440 | tf_op jit(solution)/shard_map/ppermute | solution.py:320
  20.7 2.8 %copy-start.1 = (bf16[48,64,1024]{2,1,0:T(8,128)(2,1)S(1)}, bf16[48,64,1024]{2,1,0:T(8,128)(2,1)}, u32[]{:S(2)}) copy-start(bf16[48,64,1024]{2,1,0:T(8,128)(2,1)} %param.16) | copy-start | bytes 18874372
  29.0 17.3 %copy-start = (bf16[8192,128]{1,0:T(8,128)(2,1)S(1)}, bf16[8192,128]{1,0:T(8,128)(2,1)}, u32[]{:S(2)}) copy-start(bf16[8192,128]{1,0:T(8,128)(2,1)} %w_ref.3) | copy-start | bytes 6291460
  32.8 0.7 copy-start.3
  34.1 18.0 %all-to-all-start.4 = ((bf16[8,144,128]{2,1,0:T(8,128)(2,1)}), bf16[8,144,128]{2,1,0:T(8,128)(2,1)S(1)}, u32[]{:S(2)}, u32[]{:S(2)}) async-start(bf16[8,144,128]{2,1,0:T(8,128)(2,1)} %copy-done.3), calls=%async_computation.4 | async-start | bytes 589824 | tf_op jit(solution)/shard_map/all_to_all | solution.py:262
  41.7 23.1 %collective-permute-start.4 = (bf16[128,1024]{1,0:T(8,128)(2,1)}, bf16[128,1024]{1,0:T(8,128)(2,1)}, u32[]{:S(2)}, u32[]{:S(2)}) collective-permute-start(bf16[128,1024]{1,0:T(8,128)(2,1)} %collective-permute-done.2.refs_3_), channel_id=1, source_target_pairs={{0,1},{1,2},{2,3},{3,4},{4,5},{5,6},{6,7},{7,0},{8,9},{9,10},{10,1... | collective-permute-start | bytes 786440 | tf_op jit(solution)/shard_map/ppermute | solution.py:320
  43.1 21.7 %collective-permute-start.5 = (bf16[128,1024]{1,0:T(8,128)(2,1)}, bf16[128,1024]{1,0:T(8,128)(2,1)}, u32[]{:S(2)}, u32[]{:S(2)}) collective-permute-start(bf16[128,1024]{1,0:T(8,128)(2,1)} %collective-permute-done.3.refs_4_), channel_id=1, source_target_pairs={{0,7},{1,0},{2,1},{3,2},{4,3},{5,4},{6,5},{7,6},{8,15},{9,8},{10,9... | collective-permute-start | bytes 786440 | tf_op jit(solution)/shard_map/ppermute | solution.py:320
  44.4 20.4 %collective-permute-start.6 = (bf16[128,1024]{1,0:T(8,128)(2,1)}, bf16[128,1024]{1,0:T(8,128)(2,1)}, u32[]{:S(2)}, u32[]{:S(2)}) collective-permute-start(bf16[128,1024]{1,0:T(8,128)(2,1)} %collective-permute-done.2.refs_3_), channel_id=1, source_target_pairs={{0,2},{1,3},{2,4},{3,5},{4,6},{5,7},{6,0},{7,1},{8,10},{9,11},{10,... | collective-permute-start | bytes 786440 | tf_op jit(solution)/shard_map/ppermute | solution.py:320
  48.1 15.8 %copy-start.2 = (bf16[48,64,128]{2,1,0:T(8,128)(2,1)S(1)}, bf16[48,64,128]{2,1,0:T(8,128)(2,1)}, u32[]{:S(2)}) copy-start(bf16[48,64,128]{2,1,0:T(8,128)(2,1)} %param.17) | copy-start | bytes 2359300
  54.4 17.1 %all-to-all-start.5 = ((bf16[32,16,128]{2,1,0:T(8,128)(2,1)}), bf16[32,16,128]{2,1,0:T(8,128)(2,1)S(1)}, u32[]{:S(2)}, u32[]{:S(2)}) async-start(bf16[32,16,128]{2,1,0:T(8,128)(2,1)} %bitcast.13), calls=%async_computation.5 | async-start | bytes 262144 | tf_op jit(solution)/shard_map/all_to_all | solution.py:262
  64.8 6.8 %copy-start.7 = (bf16[16,64,128]{2,1,0:T(8,128)(2,1)S(1)}, bf16[16,64,128]{2,1,0:T(8,128)(2,1)}, u32[]{:S(2)}) copy-start(bf16[16,64,128]{2,1,0:T(8,128)(2,1)} %param.15) | copy-start | bytes 786436
